TPU v7x, 128 devices: a whole 4x4x4 slice. The times are simulated.
128 devices in a mesh: mesh: 16 (over y, x), span: 8 (over z, core).
Axes of the slice: x: 4, y: 4, z: 4, core: 2. Of those that a mesh axis runs over, the one named last changes fastest.
Arguments:
- velocity_q: float32 [512, 49, 2048], P('span', None, 'mesh'), may hold values from -6 to 6
- advecting: bfloat16 [2, 512, 49, 2048], P(None, 'span', None, 'mesh'), may hold values from -0.01171875 to 0.01171875
- damping: float32 [49, 2048], P(None, 'mesh'), may hold values from 0.02 to 8
Outputs:
- q_new: float32 [512, 49, 2048], P('span', None, 'mesh')
All inputs are finite; a program needn't handle non-finite values.
Results may differ from a plain program's by a relative error of at most 0.0003.
Values sent between devices are 32-bit elements; how exact they have to be, the bound alone decides.
No kernel may reach another device: no remote copies, remote signals or barrier semaphores. Data moves between devices by JAX's collectives and lax.ppermute only.
A program may use at most 128 MiB of HBM per device.

v0:
```python
from functools import partial
import math

import jax
import jax.numpy as jnp
import numpy as np
from jax import lax
from jax.sharding import PartitionSpec as P

ORDER = 6
K_DEV = 21
ITERS = 8


LAMBDA0 = 0.1
VISCOSITY = 0.02
PENALTY = 100.0
BETA = 0.02
HIGH = lax.Precision.HIGHEST


def with_halo(array, sides, width):
    for axis, dim in sides:
        peers, length = (lax.axis_size(axis), array.shape[dim])
        up = [(i, (i + 1) % peers) for i in range(peers - 1)]
        down = [(j, i) for i, j in up]
        last = lax.slice_in_dim(array, length - width, length, axis=dim)
        leading = lax.slice_in_dim(array, 0, width, axis=dim)
        before = lax.ppermute(last, axis, up)
        after = lax.ppermute(leading, axis, down)
        array = jnp.concatenate([before, array, after], axis=dim)
    return array


def gll_tables(degree):
    side_nodes = degree + 1
    points = [-math.cos(math.pi * node_index / degree) for node_index in range(side_nodes)]
    values = [1.0] * side_nodes
    for sweep_index in range(60):
        updated = []
        new_values = []
        for node_point in points:
            lower_poly = 1.0
            legendre_now = node_point
            for order_step in range(2, degree + 1):
                next_poly = (
                    (2 * order_step - 1) * node_point * legendre_now - (order_step - 1) * lower_poly
                ) / order_step
                lower_poly = legendre_now
                legendre_now = next_poly
            updated.append(
                node_point - (node_point * legendre_now - lower_poly) / (side_nodes * legendre_now)
            )
            new_values.append(legendre_now)
        points = updated
        values = new_values
    weights = [2.0 / (degree * side_nodes * entry_value * entry_value) for entry_value in values]
    derivative = np.zeros((side_nodes, side_nodes))
    for row_index in range(side_nodes):
        for col_index in range(side_nodes):
            if row_index != col_index:
                derivative[row_index, col_index] = values[row_index] / (
                    values[col_index] * (points[row_index] - points[col_index])
                )
    derivative[0, 0] = -degree * side_nodes / 4.0
    derivative[degree, degree] = degree * side_nodes / 4.0
    return (jnp.asarray(np.array(weights), jnp.float32), jnp.asarray(derivative, jnp.float32))


def fourier_table(number, planes, wave_count):
    coeff_index = jnp.arange(number, dtype=jnp.int32)[:, None]
    plane_index = jnp.arange(planes, dtype=jnp.int32)[None, :]
    cosine = coeff_index < wave_count
    wavenumber = jnp.where(cosine, coeff_index, coeff_index - wave_count + 1)
    phases = (wavenumber * plane_index % planes).astype(jnp.float32) * (2.0 * math.pi / planes)
    return jnp.where(cosine, jnp.cos(phases), jnp.sin(phases))


def along_first(derivative, values):
    return jnp.einsum("ia,maje->mije", derivative, values, precision=HIGH)


def along_second(derivative, values):
    return jnp.einsum("jb,mibe->mije", derivative, values, precision=HIGH)


def face_terms(
    first_value,
    last_value,
    first_slope,
    last_slope,
    before_value,
    before_slope,
    after_value,
    after_slope,
    weights,
    derivative,
    degree,
):
    face_weight = weights[None, :, None]
    jump_after = last_value - after_value
    jump_before = before_value - first_value
    coef_after = face_weight * (PENALTY * jump_after - 0.5 * (last_slope + after_slope))
    coef_before = face_weight * (PENALTY * jump_before - 0.5 * (before_slope + first_slope))
    spread = -0.5 * (
        jnp.einsum("a,mje->maje", derivative[degree], face_weight * jump_after, precision=HIGH)
        + jnp.einsum("a,mje->maje", derivative[0], face_weight * jump_before, precision=HIGH)
    )
    spread = spread.at[:, degree].add(coef_after)
    spread = spread.at[:, 0].add(-coef_before)
    return spread


def helmholtz(mode_field, shifts, damping, weights, derivative, degree):
    mass_weights = (weights[:, None] * weights[None, :])[:, :, None]
    grad_x = along_first(derivative, mode_field)
    grad_y = along_second(derivative, mode_field)
    first_value = mode_field[:, 0]
    last_value = mode_field[:, degree]
    first_slope = grad_x[:, 0]
    last_slope = grad_x[:, degree]
    face_stack = jnp.stack(
        [jnp.stack([first_value, first_slope]), jnp.stack([last_value, last_slope])]
    )
    slab_shape = face_stack.shape[1:]
    padded = with_halo(face_stack.reshape(2, -1), (("mesh", 0),), 1)
    before_side = padded[0].reshape(slab_shape)
    after_side = padded[3].reshape(slab_shape)
    result = jnp.einsum("ai,maje->mije", derivative, mass_weights * grad_x, precision=HIGH)
    result = result + jnp.einsum("bj,mibe->mije", derivative, mass_weights * grad_y, precision=HIGH)
    result = result + (shifts[:, None, None, None] + damping) * mass_weights * mode_field
    low_value = mode_field[:, :, 0]
    high_value = mode_field[:, :, degree]
    low_slope = grad_y[:, :, 0]
    high_slope = grad_y[:, :, degree]
    y_terms = face_terms(
        low_value,
        high_value,
        low_slope,
        high_slope,
        jnp.roll(high_value, 1, axis=2),
        jnp.roll(high_slope, 1, axis=2),
        jnp.roll(low_value, -1, axis=2),
        jnp.roll(low_slope, -1, axis=2),
        weights,
        derivative,
        degree,
    )
    result = result + jnp.swapaxes(y_terms, 1, 2)
    x_terms = face_terms(
        first_value,
        last_value,
        first_slope,
        last_slope,
        before_side[0],
        before_side[1],
        after_side[0],
        after_side[1],
        weights,
        derivative,
        degree,
    )
    return result + x_terms


def inner_sums(left_field, right_field):
    return jnp.sum(left_field * right_field, axis=(1, 2, 3))


def per_mode(vector):
    return vector[:, None, None, None]


def guarded(active, values):
    return jnp.where(active, values, 1.0)


def squared_norm(residual):
    return lax.psum(inner_sums(residual, residual), "mesh")


def body(velocity_q, advecting, damping):
    degree = ORDER
    side_nodes = degree + 1
    weights, derivative = gll_tables(degree)
    span_size = lax.axis_size("span")
    plane_count = velocity_q.shape[0]
    column_count = velocity_q.shape[2]
    total_planes = plane_count * span_size
    wave_count = K_DEV * span_size
    kept_count = 2 * wave_count
    local_q = velocity_q.reshape(plane_count, side_nodes, side_nodes, column_count)
    edge_weight = weights[0]
    first_face = local_q[:, 0]
    last_face = local_q[:, degree]
    edge_traces = with_halo(
        jnp.stack([first_face, last_face], axis=1).reshape(plane_count, 2, -1), (("mesh", 1),), 1
    )
    grad_x = along_first(derivative, local_q)
    grad_y = along_second(derivative, local_q)
    low_side = local_q[:, :, 0]
    high_side = local_q[:, :, degree]
    grad_y = grad_y.at[:, :, degree].add(
        (jnp.roll(low_side, -1, axis=2) - high_side) / (2.0 * edge_weight)
    )
    grad_y = grad_y.at[:, :, 0].add(
        -(jnp.roll(high_side, 1, axis=2) - low_side) / (2.0 * edge_weight)
    )
    from_left = edge_traces[:, 0].reshape(first_face.shape)
    from_right = edge_traces[:, 3].reshape(first_face.shape)
    grad_x = grad_x.at[:, degree].add((from_right - last_face) / (2.0 * edge_weight))
    grad_x = grad_x.at[:, 0].add(-(from_left - first_face) / (2.0 * edge_weight))
    velocity = advecting.astype(jnp.float32).reshape(
        2, plane_count, side_nodes, side_nodes, column_count
    )
    forcing = LAMBDA0 * local_q - (velocity[0] * grad_x + velocity[1] * grad_y) / VISCOSITY
    columns = lax.all_to_all(
        forcing.reshape(plane_count, -1), "span", split_axis=1, concat_axis=0, tiled=True
    )
    basis_table = fourier_table(total_planes, total_planes, wave_count)
    coeff_index = jnp.arange(total_planes, dtype=jnp.int32)
    scaling = jnp.where(coeff_index == 0, 1.0 / total_planes, 2.0 / total_planes).astype(
        jnp.float32
    )
    spectra = jnp.dot(
        basis_table * scaling[:, None], columns, precision=HIGH, preferred_element_type=jnp.float32
    )
    spectra = spectra * (coeff_index < kept_count).astype(jnp.float32)[:, None]
    local_spectra = lax.all_to_all(spectra, "span", split_axis=0, concat_axis=1, tiled=True)
    mode_count = total_planes // span_size
    my_index = lax.axis_index("span") * mode_count + jnp.arange(mode_count, dtype=jnp.int32)
    my_wave = jnp.where(my_index < wave_count, my_index, my_index - wave_count + 1).astype(
        jnp.float32
    )
    shifts = LAMBDA0 + (BETA * my_wave) ** 2
    active = my_index < kept_count
    mass_weights = (weights[:, None] * weights[None, :])[:, :, None]
    right_side = mass_weights * local_spectra.reshape(
        mode_count, side_nodes, side_nodes, column_count
    )
    damp_nodes = damping.reshape(side_nodes, side_nodes, column_count)
    operate = partial(
        helmholtz,
        shifts=shifts,
        damping=damp_nodes,
        weights=weights,
        derivative=derivative,
        degree=degree,
    )
    solution = jnp.zeros_like(right_side)
    residual = right_side
    direction = right_side
    res_norm = squared_norm(residual)
    for iteration in range(ITERS):
        operated = operate(direction)
        curve_sum = lax.psum(inner_sums(direction, operated), "mesh")
        step_size = res_norm / guarded(active, curve_sum)
        solution = solution + per_mode(step_size) * direction
        residual = residual - per_mode(step_size) * operated
        new_norm = squared_norm(residual)
        conj_ratio = new_norm / guarded(active, res_norm)
        direction = residual + per_mode(conj_ratio) * direction
        res_norm = new_norm
    gathered = lax.all_to_all(
        solution.reshape(mode_count, -1), "span", split_axis=1, concat_axis=0, tiled=True
    )
    physical = jnp.dot(basis_table.T, gathered, precision=HIGH, preferred_element_type=jnp.float32)
    planes_back = lax.all_to_all(physical, "span", split_axis=0, concat_axis=1, tiled=True)
    return planes_back.reshape(plane_count, side_nodes * side_nodes, column_count)


def solution(mesh):
    placed = (P("span", None, "mesh"), P(None, "span", None, "mesh"), P(None, "mesh"))
    return jax.shard_map(
        body, mesh=mesh, in_specs=placed, out_specs=P("span", None, "mesh"), check_vma=False
    )
```

profile of v0, /device:TPU:1, one launch (start us, length us, event | category | flops | bytes accessed | tf_op | source)
XLA Modules:
  0.0 1350.6 jit_solution(17098240728865027538)
XLA Ops:
  23.8 7.2 all-to-all-start
  31.0 23.4 %all-to-all-done = f32[64,8,784]{2,0,1:T(8,128)S(1)} async-done(((f32[64,8,784]{2,0,1:T(8,128)}), f32[64,8,784]{2,0,1:T(8,128)S(1)}, u32[]{:S(2)}, u32[]{:S(2)}) %all-to-all-start) | async-done | bytes 1605664 | tf_op jit(solution)/shard_map/all_to_all | solution.py:217
  54.5 10.7 convolution_multiply_fusion
  72.7 22.2 %all-to-all-done.1 = f32[8,64,784]{2,1,0:T(8,128)S(1)} async-done(((f32[8,64,784]{2,1,0:T(8,128)}), f32[8,64,784]{2,1,0:T(8,128)S(1)}, u32[]{:S(2)}, u32[]{:S(2)}) %all-to-all-start.1) | async-done | bytes 1605664 | tf_op jit(solution)/shard_map/all_to_all | solution.py:229
  121.4 12.0 collective-permute-start.2
  189.5 32.7 %all-reduce = (f32[64]{0:T(128)S(1)}, f32[64]{0:T(128)S(1)}) all-reduce(f32[64]{0:T(128)S(1)} %multiply_reduce_fusion, f32[64]{0:T(128)S(1)} %fusion.90), channel_id=1, replica_groups=mesh['mesh'=16,'span'=8] {'mesh'}, use_global_device_ids=true, to_apply=%region_1.2 | all-reduce | flops 128 | bytes 1024 | tf_op jit(solution)/shard_map/psum | solution.py:179
  224.0 28.7 %psum.114 = f32[64]{0:T(128)S(1)} all-reduce(f32[64]{0:T(128)S(1)} %get-tuple-element.527), channel_id=1, replica_groups=mesh['mesh'=16,'span'=8] {'mesh'}, use_global_device_ids=true, to_apply=%region_5.6 | all-reduce | flops 64 | bytes 512 | tf_op jit(solution)/shard_map/psum | solution.py:179
  313.9 29.2 %psum.115 = f32[64]{0:T(128)S(1)} all-reduce(f32[64]{0:T(128)S(1)} %get-tuple-element.521), channel_id=1, replica_groups=mesh['mesh'=16,'span'=8] {'mesh'}, use_global_device_ids=true, to_apply=%region_7.8 | all-reduce | flops 64 | bytes 512 | tf_op jit(solution)/shard_map/psum | solution.py:256
  346.3 29.9 %psum.116 = f32[64]{0:T(128)S(1)} all-reduce(f32[64]{0:T(128)S(1)} %get-tuple-element.519), channel_id=1, replica_groups=mesh['mesh'=16,'span'=8] {'mesh'}, use_global_device_ids=true, to_apply=%region_9.10 | all-reduce | flops 64 | bytes 512 | tf_op jit(solution)/shard_map/psum | solution.py:179
  437.4 28.5 %psum.117 = f32[64]{0:T(128)S(1)} all-reduce(f32[64]{0:T(128)S(1)} %get-tuple-element.513), channel_id=1, replica_groups=mesh['mesh'=16,'span'=8] {'mesh'}, use_global_device_ids=true, to_apply=%region_11.12 | all-reduce | flops 64 | bytes 512 | tf_op jit(solution)/shard_map/psum | solution.py:256
  469.0 30.3 %psum.118 = f32[64]{0:T(128)S(1)} all-reduce(f32[64]{0:T(128)S(1)} %get-tuple-element.511), channel_id=1, replica_groups=mesh['mesh'=16,'span'=8] {'mesh'}, use_global_device_ids=true, to_apply=%region_13.14 | all-reduce | flops 64 | bytes 512 | tf_op jit(solution)/shard_map/psum | solution.py:179
  574.5 28.5 %psum.119 = f32[64]{0:T(128)S(1)} all-reduce(f32[64]{0:T(128)S(1)} %get-tuple-element.505), channel_id=1, replica_groups=mesh['mesh'=16,'span'=8] {'mesh'}, use_global_device_ids=true, to_apply=%region_15.16 | all-reduce | flops 64 | bytes 512 | tf_op jit(solution)/shard_map/psum | solution.py:256
  606.7 30.6 %psum.120 = f32[64]{0:T(128)S(1)} all-reduce(f32[64]{0:T(128)S(1)} %get-tuple-element.503), channel_id=1, replica_groups=mesh['mesh'=16,'span'=8] {'mesh'}, use_global_device_ids=true, to_apply=%region_17.18 | all-reduce | flops 64 | bytes 512 | tf_op jit(solution)/shard_map/psum | solution.py:179
  714.3 28.5 %psum.121 = f32[64]{0:T(128)S(1)} all-reduce(f32[64]{0:T(128)S(1)} %get-tuple-element.497), channel_id=1, replica_groups=mesh['mesh'=16,'span'=8] {'mesh'}, use_global_device_ids=true, to_apply=%region_19.20 | all-reduce | flops 64 | bytes 512 | tf_op jit(solution)/shard_map/psum | solution.py:256
  746.6 30.2 %psum.122 = f32[64]{0:T(128)S(1)} all-reduce(f32[64]{0:T(128)S(1)} %get-tuple-element.495), channel_id=1, replica_groups=mesh['mesh'=16,'span'=8] {'mesh'}, use_global_device_ids=true, to_apply=%region_21.22 | all-reduce | flops 64 | bytes 512 | tf_op jit(solution)/shard_map/psum | solution.py:179
  851.7 28.5 %psum.123 = f32[64]{0:T(128)S(1)} all-reduce(f32[64]{0:T(128)S(1)} %get-tuple-element.489), channel_id=1, replica_groups=mesh['mesh'=16,'span'=8] {'mesh'}, use_global_device_ids=true, to_apply=%region_23.24 | all-reduce | flops 64 | bytes 512 | tf_op jit(solution)/shard_map/psum | solution.py:256
  882.6 30.5 %psum.124 = f32[64]{0:T(128)S(1)} all-reduce(f32[64]{0:T(128)S(1)} %multiply_reduce_fusion.3), channel_id=1, replica_groups=mesh['mesh'=16,'span'=8] {'mesh'}, use_global_device_ids=true, to_apply=%region_25.26 | all-reduce | flops 64 | bytes 512 | tf_op jit(solution)/shard_map/psum | solution.py:179
  999.0 28.6 %psum.125 = f32[64]{0:T(128)S(1)} all-reduce(f32[64]{0:T(128)S(1)} %multiply_reduce_fusion.2), channel_id=1, replica_groups=mesh['mesh'=16,'span'=8] {'mesh'}, use_global_device_ids=true, to_apply=%region_27.28 | all-reduce | flops 64 | bytes 512 | tf_op jit(solution)/shard_map/psum | solution.py:256
  1032.0 30.0 %psum.126 = f32[64]{0:T(128)S(1)} all-reduce(f32[64]{0:T(128)S(1)} %get-tuple-element.483), channel_id=1, replica_groups=mesh['mesh'=16,'span'=8] {'mesh'}, use_global_device_ids=true, to_apply=%region_29.30 | all-reduce | flops 64 | bytes 512 | tf_op jit(solution)/shard_map/psum | solution.py:179
  1129.0 31.9 %psum.127 = f32[64]{0:T(128)S(1)} all-reduce(f32[64]{0:T(128)S(1)} %fusion.70), channel_id=1, replica_groups=mesh['mesh'=16,'span'=8] {'mesh'}, use_global_device_ids=true, to_apply=%region_31.32 | all-reduce | flops 64 | bytes 512 | tf_op jit(solution)/shard_map/psum | solution.py:256
  1169.3 116.5 %all-to-all-start.2 = ((f32[64,8,784]{2,0,1:T(8,128)}), f32[64,8,784]{2,0,1:T(8,128)S(1)}, u32[]{:S(2)}, u32[]{:S(2)}) async-start(f32[64,8,784]{2,0,1:T(8,128)} %copy.3048), calls=%async_computation.2 | async-start | bytes 3670016 | tf_op jit(solution)/shard_map/all_to_all | solution.py:264
  1285.8 23.5 %all-to-all-done.2 = f32[64,8,784]{2,0,1:T(8,128)S(1)} async-done(((f32[64,8,784]{2,0,1:T(8,128)}), f32[64,8,784]{2,0,1:T(8,128)S(1)}, u32[]{:S(2)}, u32[]{:S(2)}) %all-to-all-start.2) | async-done | bytes 1605664 | tf_op jit(solution)/shard_map/all_to_all | solution.py:264
  1309.4 7.6 fusion.104
  1317.0 27.1 %all_to_all.67 = f32[8,64,784]{2,1,0:T(8,128)S(1)} all-to-all(f32[8,64,784]{2,1,0:T(8,128)S(1)} %fusion.104), channel_id=1, replica_groups=mesh['mesh'=16,'span'=8] {'span'}, dimensions={0} | all-to-all | bytes 3211264 | tf_op jit(solution)/shard_map/all_to_all | solution.py:268
  (795 shorter events, 650.9 us)
Async XLA Ops:
  1.3 14.8 %collective-permute-start = (f32[64,1,896]{2,0,1:T(8,128)S(1)}, f32[64,1,896]{2,0,1:T(8,128)S(1)}, u32[]{:S(2)}, u32[]{:S(2)}) collective-permute-start(f32[64,1,896]{2,0,1:T(8,128)S(1)} %get-tuple-element.639), channel_id=1, source_target_pairs={{8,0},{16,8},{24,16},{32,24},{40,32},{48,40},{56,48},{64,56},{72,6... | collective-permute-start | bytes 688136 | tf_op jit(solution)/shard_map/ppermute | solution.py:30
  2.6 13.6 %collective-permute-start.1 = (f32[64,1,896]{2,0,1:T(8,128)S(1)}, f32[64,1,896]{2,0,1:T(8,128)S(1)}, u32[]{:S(2)}, u32[]{:S(2)}) collective-permute-start(f32[64,1,896]{2,0,1:T(8,128)S(1)} %get-tuple-element.638), channel_id=1, source_target_pairs={{0,8},{8,16},{16,24},{24,32},{32,40},{40,48},{48,56},{56,64},{64,7... | collective-permute-start | bytes 688136 | tf_op jit(solution)/shard_map/ppermute | solution.py:29
  23.8 30.7 %all-to-all-start = ((f32[64,8,784]{2,0,1:T(8,128)}), f32[64,8,784]{2,0,1:T(8,128)S(1)}, u32[]{:S(2)}, u32[]{:S(2)}) async-start(f32[64,8,784]{2,0,1:T(8,128)} %copy.2710), calls=%async_computation | async-start | bytes 3670016 | tf_op jit(solution)/shard_map/all_to_all | solution.py:217
  66.9 28.0 %all-to-all-start.1 = ((f32[8,64,784]{2,1,0:T(8,128)}), f32[8,64,784]{2,1,0:T(8,128)S(1)}, u32[]{:S(2)}, u32[]{:S(2)}) async-start(f32[8,64,784]{2,1,0:T(8,128)} %bitcast.1330), calls=%async_computation.1 | async-start | bytes 3670016 | tf_op jit(solution)/shard_map/all_to_all | solution.py:229
  101.1 121.2 %copy-start.3 = (f32[64,7,7,128]{3,2,1,0:T(8,128)}, f32[64,7,7,128]{3,2,1,0:T(8,128)S(1)}, u32[]{:S(2)}) copy-start(f32[64,7,7,128]{3,2,1,0:T(8,128)S(1)} %reshape.2520) | copy-start | bytes 4816900
  121.4 20.6 %collective-permute-start.2 = (f32[1,114688]{1,0:T(1,128)}, f32[1,114688]{1,0:T(1,128)S(1)}, u32[]{:S(2)}, u32[]{:S(2)}) collective-permute-start(f32[1,114688]{1,0:T(1,128)} %slice.1665), channel_id=1, source_target_pairs={{8,0},{16,8},{24,16},{32,24},{40,32},{48,40},{56,48},{64,56},{72,6... | collective-permute-start | bytes 1376264 | tf_op jit(solution)/shard_map/ppermute | solution.py:30
  151.7 15.1 %collective-permute-start.3 = (f32[1,114688]{1,0:T(1,128)}, f32[1,114688]{1,0:T(1,128)}, u32[]{:S(2)}, u32[]{:S(2)}) collective-permute-start(f32[1,114688]{1,0:T(1,128)} %slice.1668), channel_id=1, source_target_pairs={{0,8},{8,16},{16,24},{24,32},{32,40},{40,48},{48,56},{56,64},{64,7... | collective-permute-start | bytes 1376264 | tf_op jit(solution)/shard_map/ppermute | solution.py:29
  271.7 9.8 collective-permute-start.4
  290.2 12.1 collective-permute-start.5
  394.3 9.8 collective-permute-start.6
  413.7 12.0 collective-permute-start.7
  519.2 11.5 collective-permute-start.8
  540.3 15.9 %collective-permute-start.9 = (f32[1,114688]{1,0:T(1,128)}, f32[1,114688]{1,0:T(1,128)}, u32[]{:S(2)}, u32[]{:S(2)}) collective-permute-start(f32[1,114688]{1,0:T(1,128)} %slice.1746), channel_id=1, source_target_pairs={{0,8},{8,16},{16,24},{24,32},{32,40},{40,48},{48,56},{56,64},{64,7... | collective-permute-start | bytes 1376264 | tf_op jit(solution)/shard_map/ppermute | solution.py:29
  657.6 12.0 collective-permute-start.10
  679.3 15.8 %collective-permute-start.11 = (f32[1,114688]{1,0:T(1,128)}, f32[1,114688]{1,0:T(1,128)}, u32[]{:S(2)}, u32[]{:S(2)}) collective-permute-start(f32[1,114688]{1,0:T(1,128)} %slice.1772), channel_id=1, source_target_pairs={{0,8},{8,16},{16,24},{24,32},{32,40},{40,48},{48,56},{56,64},{64,7... | collective-permute-start | bytes 1376264 | tf_op jit(solution)/shard_map/ppermute | solution.py:29
  797.9 26.7 %collective-permute-start.12 = (f32[1,114688]{1,0:T(1,128)}, f32[1,114688]{1,0:T(1,128)}, u32[]{:S(2)}, u32[]{:S(2)}) collective-permute-start(f32[1,114688]{1,0:T(1,128)} %slice.1795), channel_id=1, source_target_pairs={{8,0},{16,8},{24,16},{32,24},{40,32},{48,40},{56,48},{64,56},{72,6... | collective-permute-start | bytes 1376264 | tf_op jit(solution)/shard_map/ppermute | solution.py:30
  803.6 27.5 %collective-permute-start.13 = (f32[1,114688]{1,0:T(1,128)}, f32[1,114688]{1,0:T(1,128)}, u32[]{:S(2)}, u32[]{:S(2)}) collective-permute-start(f32[1,114688]{1,0:T(1,128)} %slice.1798), channel_id=1, source_target_pairs={{0,8},{8,16},{16,24},{24,32},{32,40},{40,48},{48,56},{56,64},{64,7... | collective-permute-start | bytes 1376264 | tf_op jit(solution)/shard_map/ppermute | solution.py:29
  939.5 14.3 %collective-permute-start.14 = (f32[1,114688]{1,0:T(1,128)}, f32[1,114688]{1,0:T(1,128)}, u32[]{:S(2)}, u32[]{:S(2)}) collective-permute-start(f32[1,114688]{1,0:T(1,128)} %slice.1821), channel_id=1, source_target_pairs={{8,0},{16,8},{24,16},{32,24},{40,32},{48,40},{56,48},{64,56},{72,6... | collective-permute-start | bytes 1376264 | tf_op jit(solution)/shard_map/ppermute | solution.py:30
  964.6 11.5 collective-permute-start.15
  1087.9 17.1 %collective-permute-start.17 = (f32[1,114688]{1,0:T(1,128)}, f32[1,114688]{1,0:T(1,128)}, u32[]{:S(2)}, u32[]{:S(2)}) collective-permute-start(f32[1,114688]{1,0:T(1,128)} %slice.1850), channel_id=1, source_target_pairs={{0,8},{8,16},{16,24},{24,32},{32,40},{40,48},{48,56},{56,64},{64,7... | collective-permute-start | bytes 1376264 | tf_op jit(solution)/shard_map/ppermute | solution.py:29
  1095.1 15.4 %collective-permute-start.16 = (f32[1,114688]{1,0:T(1,128)}, f32[1,114688]{1,0:T(1,128)}, u32[]{:S(2)}, u32[]{:S(2)}) collective-permute-start(f32[1,114688]{1,0:T(1,128)} %slice.1847), channel_id=1, source_target_pairs={{8,0},{16,8},{24,16},{32,24},{40,32},{48,40},{56,48},{64,56},{72,6... | collective-permute-start | bytes 1376264 | tf_op jit(solution)/shard_map/ppermute | solution.py:30
  1169.3 140.1 %copy-start.166 = (s32[512]{0:T(512)S(1)}, s32[512]{0:T(512)}, u32[]{:S(2)}) copy-start(s32[512]{0:T(512)} %copy-done.165) | copy-start | bytes 6148
  1169.3 140.1 %copy-start.168 = (pred[512]{0:T(512)(128)(4,1)S(1)}, pred[512]{0:T(512)(128)(4,1)}, u32[]{:S(2)}) copy-start(pred[512]{0:T(512)(128)(4,1)} %copy-done.167) | copy-start | bytes 1540
  1169.3 140.1 %all-to-all-start.2 = ((f32[64,8,784]{2,0,1:T(8,128)}), f32[64,8,784]{2,0,1:T(8,128)S(1)}, u32[]{:S(2)}, u32[]{:S(2)}) async-start(f32[64,8,784]{2,0,1:T(8,128)} %copy.3048), calls=%async_computation.2 | async-start | bytes 3670016 | tf_op jit(solution)/shard_map/all_to_all | solution.py:264
  (166 other events, 815.9 us)
where the time goes:
time: 1360 us; the launch traced here: 1350 us
  blocking collectives  474 us (35%)
  local copies, waits for them, and re-layouts  260 us (19%)
  other arithmetic  219 us (16%)
  starting transfers between devices  195 us (14%)
  matrix products  131 us (10%)
  waiting for transfers between devices  69.5 us (5%)
    psum x8, blocking collectives, squared_norm(): return lax.psum(inner_sums(residual, residual), 'mesh')  243 us
    psum x7, blocking collectives, body(): curve_sum = lax.psum(inner_sums(direction, operated), 'mesh')  204 us
    all_to_all x1, starting transfers between devices, body(): lax.all_to_all(solution.reshape(mode_count, -1), 'span', split_axis=1, co...  117 us
    reduce_sum x16, other arithmetic, inner_sums(): return jnp.sum(left_field * right_field, axis=(1, 2, 3))  46.3 us
    ppermute x9, starting transfers between devices, with_halo(): before = lax.ppermute(last, axis, up)  42.3 us
    dot_general x8, matrix products, helmholtz(): jnp.einsum('bj,mibe->mije', derivative, mass_weights * grad_y, precision=...  32.1 us
    dot_general x8, matrix products, helmholtz(): jnp.einsum('ai,maje->mije', derivative, mass_weights * grad_x, precision=...  31.1 us
    slice x8, other arithmetic, helmholtz(): before_side[0]  30.4 us
  transfers between devices with their start and end apart: 21, of which 4 were waited for; matrix products, arithmetic and copies ran while one was open for 12% of the time, Pallas kernels for 0%

commit v1 on v0

v1 whole, which is shorter than its diff:
```python
import math

import jax
import jax.numpy as jnp
import ml_dtypes
import numpy as np
from jax import lax
from jax.experimental import pallas as pl
from jax.experimental.pallas import tpu as pltpu
from jax.sharding import PartitionSpec as P

ORDER = 6
SIDE = 7
NODES = 49
EY = 128
COLS = 16
PLANES = 512
PL_DEV = 64
N_SPAN = 8
N_DEV = 128
WAVES = 168
KEPT = 336
M_DEV = 3
M_ALL = N_DEV * M_DEV
SHARE = 8 * EY
ITERS = 8

LAMBDA0 = 0.1
VISCOSITY = 0.02
PENALTY = 100.0
BETA = 0.02
VMEM = 56 * 1024 * 1024


def gll_tables(degree):
    side_nodes = degree + 1
    points = [-math.cos(math.pi * n / degree) for n in range(side_nodes)]
    values = [1.0] * side_nodes
    for _ in range(60):
        updated = []
        new_values = []
        for point in points:
            lower = 1.0
            now = point
            for step in range(2, degree + 1):
                lower, now = now, ((2 * step - 1) * point * now - (step - 1) * lower) / step
            updated.append(point - (point * now - lower) / (side_nodes * now))
            new_values.append(now)
        points = updated
        values = new_values
    weights = np.array([2.0 / (degree * side_nodes * v * v) for v in values])
    derivative = np.zeros((side_nodes, side_nodes))
    for row in range(side_nodes):
        for col in range(side_nodes):
            if row != col:
                derivative[row, col] = values[row] / (values[col] * (points[row] - points[col]))
    derivative[0, 0] = -degree * side_nodes / 4.0
    derivative[degree, degree] = degree * side_nodes / 4.0
    return weights, derivative


W, D = gll_tables(ORDER)


def fourier_table():
    c = np.arange(M_ALL)[:, None]
    p = np.arange(PLANES)[None, :]
    k = np.where(c < WAVES, c, c - WAVES + 1)
    phases = ((k * p) % PLANES) * (2.0 * math.pi / PLANES)
    table = np.where(c < WAVES, np.cos(phases), np.sin(phases))
    return np.where(c < KEPT, table, 0.0)


def in_two(table):
    table = table.astype(np.float32)
    high = table.astype(ml_dtypes.bfloat16)
    low = (table - high.astype(np.float32)).astype(ml_dtypes.bfloat16)
    return jnp.asarray(high), jnp.asarray(low)


def split(x):
    high = x.astype(jnp.bfloat16)
    low = (x - high.astype(jnp.float32)).astype(jnp.bfloat16)
    return high, low


def dot(a, b):
    return jnp.dot(a, b, preferred_element_type=jnp.float32)


def combine(coefs, values):
    total = None
    for c, v in zip(coefs, values):
        if c == 0.0:
            continue
        term = v * np.float32(c)
        total = term if total is None else total + term
    return total


def forcing_kernel(q_ref, left_ref, right_ref, a_ref, out_ref):
    table = D / VISCOSITY
    edge = 1.0 / (2.0 * W[0] * VISCOSITY)
    own = table.copy()
    own[6, 6] -= edge
    own[0, 0] += edge
    edge = np.float32(edge)

    def block(b, carry):
        rows = pl.ds(pl.multiple_of(b * 16, 16), 16)
        for i in range(SIDE):
            line = [q_ref[i * SIDE + j, rows, :] for j in range(SIDE)]
            gy = [combine(own[j], line) for j in range(SIDE)]
            gy[6] = gy[6] + edge * pltpu.roll(line[0], EY - 1, 1)
            gy[0] = gy[0] - edge * pltpu.roll(line[6], 1, 1)
            for j in range(SIDE):
                gx = combine(own[i], [q_ref[a * SIDE + j, rows, :] for a in range(SIDE)])
                if i == 6:
                    gx = gx + edge * right_ref[j, rows, :]
                if i == 0:
                    gx = gx - edge * left_ref[j, rows, :]
                n = i * SIDE + j
                ax = a_ref[0, n, rows, :].astype(jnp.float32)
                ay = a_ref[1, n, rows, :].astype(jnp.float32)
                out_ref[i, rows, j * EY : (j + 1) * EY] = (
                    np.float32(LAMBDA0) * line[j] - (ax * gx + ay * gy[j])
                )
        return carry

    lax.fori_loop(0, PL_DEV // 16, block, 0)
    out_ref[7] = jnp.zeros((PL_DEV, SIDE * EY), jnp.float32)


def forward_kernel(x_ref, high_ref, low_ref, out_ref):
    for start, width in ((0, 2), (2, 2), (4, 2), (6, 1)):
        x = x_ref[:, start * EY : (start + width) * EY]
        xh, xl = split(x)
        res = dot(high_ref[...], xh) + (dot(high_ref[...], xl) + dot(low_ref[...], xh))
        for g in range(width):
            out_ref[pl.ds(start + g, M_ALL, stride=8), :] = res[:, g * EY : (g + 1) * EY]
    out_ref[pl.ds(7, M_ALL, stride=8), :] = jnp.zeros((M_ALL, EY), jnp.float32)


def inverse_kernel(x_ref, high_ref, low_ref, out_ref):
    for start, width in ((0, 2), (2, 2), (4, 2), (6, 1)):
        x = jnp.concatenate(
            [x_ref[pl.ds(start + g, M_ALL, stride=8), :] for g in range(width)], axis=1
        )
        xh, xl = split(x)
        res = dot(high_ref[...], xh) + (dot(high_ref[...], xl) + dot(low_ref[...], xh))
        out_ref[:, start * EY : (start + width) * EY] = res


def solve_tables():
    own = D.T @ np.diag(W) @ D
    own[6, 6] += PENALTY
    own[6, :] -= D[6, :] / 2
    own[:, 6] -= D[6, :] / 2
    own[0, 0] += PENALTY
    own[0, :] += D[0, :] / 2
    own[:, 0] += D[0, :] / 2
    return own


OWN = solve_tables()


def line_image(v, from_next, from_before):
    even = [v[0] + v[6], v[1] + v[5], v[2] + v[4], v[3]]
    odd = [v[0] - v[6], v[1] - v[5], v[2] - v[4]]
    d6 = D[6]
    d_even = [(d6[a] + d6[6 - a]) / 2 for a in range(3)] + [d6[3]]
    d_odd = [(d6[a] - d6[6 - a]) / 2 for a in range(3)]
    half_even = combine([c / 2 for c in d_even], even)
    half_odd = combine([c / 2 for c in d_odd], odd)
    penalty = np.float32(PENALTY)
    first = penalty * v[0] + (half_odd - half_even)
    last = penalty * v[6] - (half_even + half_odd)
    next_value = from_next(v[0])
    next_first = from_next(first)
    before_value = from_before(v[6])
    before_last = from_before(last)
    sum_value = next_value + before_value
    dif_value = next_value - before_value
    out = [None] * SIDE
    for i in range(3):
        e = combine(
            [(OWN[i, a] + OWN[i, 6 - a]) / 2 for a in range(3)] + [OWN[i, 3], d_even[i] / 2],
            even + [sum_value],
        )
        o = combine(
            [(OWN[i, a] - OWN[i, 6 - a]) / 2 for a in range(3)] + [d_odd[i] / 2],
            odd + [dif_value],
        )
        out[i] = e + o
        out[6 - i] = e - o
    out[3] = combine([OWN[3, a] for a in range(4)] + [d6[3] / 2], even + [sum_value])
    out[6] = out[6] - next_first
    out[0] = out[0] - before_last
    return out


def whole_sum(x):
    return jnp.sum(jnp.sum(x, axis=0, keepdims=True), axis=1, keepdims=True)


def solve_kernel(shift_ref, idle_ref, b_ref, damp_ref, out_ref, mass_ref, x_ref, r_ref, p_ref, q_ref):
    stride = N_SPAN * M_DEV * 8
    column = lax.broadcasted_iota(jnp.int32, (COLS, EY), 0)
    not_last = column < COLS - 1
    not_first = column > 0

    def x_next(v):
        return jnp.where(not_last, pltpu.roll(v, COLS - 1, 0), 0.0)

    def x_before(v):
        return jnp.where(not_first, pltpu.roll(v, 1, 0), 0.0)

    def y_next(v):
        return pltpu.roll(v, EY - 1, 1)

    def y_before(v):
        return pltpu.roll(v, 1, 1)

    zero = jnp.zeros((COLS, EY), jnp.float32)

    def one_mode(mode, carry):
        shift = shift_ref[mode]
        idle = idle_ref[mode]
        norm = zero
        for i in range(SIDE):
            for j in range(SIDE):
                n = i * SIDE + j
                w = np.float32(W[i] * W[j])
                rows = b_ref[pl.ds(i * M_DEV * 8 + mode * 8 + j, COLS, stride=stride), :]
                rhs = w * rows
                r_ref[n] = rhs
                p_ref[n] = zero
                x_ref[n] = zero
                mass_ref[n] = w * (damp_ref[n] + shift)
                norm = norm + rhs * rhs
        norm = whole_sum(norm)

        def iteration(step, state):
            norm, ratio = state
            for j in range(SIDE):
                line = []
                for i in range(SIDE):
                    n = i * SIDE + j
                    p = r_ref[n] + ratio * p_ref[n]
                    p_ref[n] = p
                    line.append(p)
                image = line_image(line, x_next, x_before)
                for i in range(SIDE):
                    n = i * SIDE + j
                    q_ref[n] = np.float32(W[j]) * image[i] + mass_ref[n] * line[i]
            curve = zero
            for i in range(SIDE):
                line = [p_ref[i * SIDE + j] for j in range(SIDE)]
                image = line_image(line, y_next, y_before)
                for j in range(SIDE):
                    n = i * SIDE + j
                    q = q_ref[n] + np.float32(W[i]) * image[j]
                    q_ref[n] = q
                    curve = curve + q * line[j]
            alpha = norm / (whole_sum(curve) + idle)
            fresh = zero
            for n in range(NODES):
                x_ref[n] = x_ref[n] + alpha * p_ref[n]
                r = r_ref[n] - alpha * q_ref[n]
                r_ref[n] = r
                fresh = fresh + r * r
            fresh = whole_sum(fresh)
            return fresh, fresh / (norm + idle)

        lax.fori_loop(0, ITERS, iteration, (norm, jnp.zeros((1, 1), jnp.float32)))
        for i in range(SIDE):
            for j in range(SIDE):
                out_ref[pl.ds(i * M_DEV * 8 + mode * 8 + j, COLS, stride=stride), :] = x_ref[i * SIDE + j]
        return carry

    lax.fori_loop(0, M_DEV, one_mode, 0)
    blank = jnp.zeros((COLS, EY), jnp.float32)
    for row in range(SIDE * M_DEV * 8, stride):
        out_ref[pl.ds(row, COLS, stride=stride), :] = blank
    for i in range(SIDE):
        for mode in range(M_DEV):
            out_ref[pl.ds(i * M_DEV * 8 + mode * 8 + 7, COLS, stride=stride), :] = blank


def call(kernel, shape, scratch=(), smem=0, n_in=0):
    full = pl.BlockSpec(memory_space=pltpu.VMEM)
    scalar = pl.BlockSpec(memory_space=pltpu.SMEM)
    return pl.pallas_call(
        kernel,
        out_shape=jax.ShapeDtypeStruct(shape, jnp.float32),
        in_specs=[scalar] * smem + [full] * n_in,
        out_specs=full,
        scratch_shapes=[pltpu.VMEM(s, jnp.float32) for s in scratch],
        compiler_params=pltpu.CompilerParams(vmem_limit_bytes=VMEM),
    )


def body(velocity_q, advecting, damping):
    everyone = ("mesh", "span")
    columns = lax.axis_size("mesh")
    up = [(i, i + 1) for i in range(columns - 1)]
    down = [(j, i) for i, j in up]
    q_nodes = jnp.transpose(velocity_q, (1, 0, 2))
    a_nodes = jnp.transpose(advecting, (0, 2, 1, 3))
    from_left = lax.ppermute(q_nodes[NODES - SIDE :], "mesh", up)
    from_right = lax.ppermute(q_nodes[:SIDE], "mesh", down)
    damp_nodes = lax.all_gather(damping, "mesh", axis=1, tiled=False)

    forcing = call(forcing_kernel, (N_SPAN, PL_DEV, SIDE * EY), n_in=4)(
        q_nodes, from_left, from_right, a_nodes
    )
    planes = lax.all_to_all(forcing, "span", split_axis=0, concat_axis=0, tiled=True)

    table = fourier_table()
    scale = np.where(np.arange(M_ALL) == 0, 1.0 / PLANES, 2.0 / PLANES)[:, None]
    spectra = call(forward_kernel, (M_ALL * 8, EY), n_in=3)(
        planes.reshape(PLANES, SIDE * EY), *in_two(table * scale)
    )
    mine = lax.all_to_all(
        spectra.reshape(N_DEV, M_DEV * 8, EY), everyone, split_axis=0, concat_axis=0, tiled=True
    )

    device = lax.axis_index("mesh") * N_SPAN + lax.axis_index("span")
    coef = device * M_DEV + jnp.arange(M_DEV, dtype=jnp.int32)
    wave = jnp.where(coef < WAVES, coef, coef - WAVES + 1).astype(jnp.float32)
    shifts = LAMBDA0 + (BETA * wave) ** 2
    idle = jnp.where(coef < KEPT, 0.0, 1.0).astype(jnp.float32)
    field = (NODES, COLS, EY)
    solved = call(
        solve_kernel, (N_DEV * M_DEV * 8, EY), scratch=(field,) * 5, smem=2, n_in=2
    )(shifts, idle, mine.reshape(N_DEV * M_DEV * 8, EY), damp_nodes)

    modes = lax.all_to_all(
        solved.reshape(N_DEV, M_DEV * 8, EY), everyone, split_axis=0, concat_axis=0, tiled=True
    )
    physical = call(inverse_kernel, (PLANES, SIDE * EY), n_in=3)(
        modes.reshape(M_ALL * 8, EY), *in_two(table.T)
    )
    back = lax.all_to_all(
        physical.reshape(N_SPAN, PL_DEV, SIDE * EY), "span", split_axis=0, concat_axis=0, tiled=True
    )
    back = back[:SIDE].reshape(SIDE, PL_DEV, SIDE, EY)
    return jnp.transpose(back, (1, 0, 2, 3)).reshape(PL_DEV, NODES, EY)


def solution(mesh):
    placed = (P("span", None, "mesh"), P(None, "span", None, "mesh"), P(None, "mesh"))
    return jax.shard_map(
        body, mesh=mesh, in_specs=placed, out_specs=P("span", None, "mesh"), check_vma=False
    )
```

time: 1360 us -> 195 us (0.14)
  blocking collectives: 474 us -> 128 us
  local copies, waits for them, and re-layouts: 260 us -> 5.56 us
  other arithmetic: 219 us -> 0.57 us
  starting transfers between devices: 195 us -> 14.9 us
  matrix products: 131 us -> 0 us
  waiting for transfers between devices: 69.5 us -> 6.75 us
  Pallas kernels: 0 us -> 37.6 us
    psum x15 -> x0, blocking collectives: 447 us -> none  [the longest x8 243 us: squared_norm(): return lax.psum(inner_sums(residual, residual), 'mesh')]
    dot_general x36 -> x0, matrix products: 131 us -> none  [the longest x8 32.1 us: helmholtz(): jnp.einsum('bj,mibe->mije', derivative, mass_weights * grad_y, precision=...]
    all_to_all x3 -> x1, starting transfers between devices: 128 us -> 9.68 us  [body(): lax.all_to_all(spectra.reshape(N_DEV, M_DEV * 8, EY), everyone, split_axi...]
    all_to_all x3 -> x1, waiting for transfers between devices: 69.1 us -> 0.01 us  [body(): lax.all_to_all(spectra.reshape(N_DEV, M_DEV * 8, EY), everyone, split_axi...]
    all_to_all x1 -> x3, blocking collectives: 27.1 us -> 96.2 us  [the longest x1 37 us: body(): lax.all_to_all(solved.reshape(N_DEV, M_DEV * 8, EY), everyone, split_axis...]
    mul x43 -> x0, other arithmetic: 65.7 us -> none  [the longest x15 25.3 us: face_terms(): face_weight * jump_after]
    slice x39 -> x2, local copies, waits for them, and re-layouts: 65 us -> 1.19 us  [the longest x1 1.08 us: body(): from_right = lax.ppermute(q_nodes[:SIDE], 'mesh', down)]
    ppermute x18 -> x2, starting transfers between devices: 66.4 us -> 5.25 us  [the longest x1 3.96 us: body(): from_left = lax.ppermute(q_nodes[NODES - SIDE:], 'mesh', up)]
  transfers between devices with their start and end apart: 21 -> 3, of which waited for: 4 -> 2; matrix products, arithmetic and copies ran while one was open for 12% -> 1% of each run, Pallas kernels for 0% -> 0%
where the time goes in v1:
time: 195 us; the launch traced here: 194 us
  blocking collectives  128 us (66%)
  Pallas kernels  37.6 us (19%)
  starting transfers between devices  14.9 us (8%)
  waiting for transfers between devices  6.75 us (3%)
  local copies, waits for them, and re-layouts  5.56 us (3%)
    all_to_all x1, blocking collectives, body(): lax.all_to_all(solved.reshape(N_DEV, M_DEV * 8, EY), everyone, split_axis...  37 us
    all_gather x1, blocking collectives, body(): damp_nodes = lax.all_gather(damping, 'mesh', axis=1, tiled=False)  32.3 us
    all_to_all x1, blocking collectives, body(): lax.all_to_all(forcing, 'span', split_axis=0, concat_axis=0, tiled=True)  30.9 us
    all_to_all x1, blocking collectives, body(): lax.all_to_all(physical.reshape(N_SPAN, PL_DEV, SIDE * EY), 'span', split...  28.4 us
    pallas_call x1, Pallas kernels, body(): call(solve_kernel, (N_DEV * M_DEV * 8, EY), scratch=(field,) * 5, smem=2,...  23.7 us
    all_to_all x1, starting transfers between devices, body(): lax.all_to_all(spectra.reshape(N_DEV, M_DEV * 8, EY), everyone, split_axi...  9.68 us
    pallas_call x1, Pallas kernels, body(): call(forcing_kernel, (N_SPAN, PL_DEV, SIDE * EY), n_in=4)  5.01 us
    pallas_call x1, Pallas kernels, body(): call(inverse_kernel, (PLANES, SIDE * EY), n_in=3)  4.59 us
  transfers between devices with their start and end apart: 3, of which 2 were waited for; matrix products, arithmetic and copies ran while one was open for 1% of the time, Pallas kernels for 0%

profile of v1, /device:TPU:1, one launch (start us, length us, event | category | flops | bytes accessed | tf_op | source)
XLA Modules:
  0.0 194.0 jit_solution(13987853483707358771)
XLA Ops:
  0.0 1.1 fusion.4
  1.1 4.0 %collective-permute-start = (f32[7,64,128]{2,1,0:T(8,128)S(1)}, f32[7,64,128]{2,1,0:T(8,128)S(1)}, u32[]{:S(2)}, u32[]{:S(2)}) collective-permute-start(f32[7,64,128]{2,1,0:T(8,128)S(1)} %get-tuple-element.6), channel_id=1, source_target_pairs={{0,8},{8,16},{16,24},{24,32},{32,40},{40,48},{48,56},{56,64},{64,7... | collective-permute-start | bytes 688136 | tf_op jit(solution)/shard_map/ppermute | solution.py:311
  5.0 1.3 collective-permute-start.1
  6.3 2.9 %collective-permute-done.left_ref = f32[7,64,128]{2,1,0:T(8,128)S(1)} collective-permute-done((f32[7,64,128]{2,1,0:T(8,128)S(1)}, f32[7,64,128]{2,1,0:T(8,128)S(1)}, u32[]{:S(2)}, u32[]{:S(2)}) %collective-permute-start) | collective-permute-done | bytes 229408 | tf_op jit(solution)/shard_map/ppermute | solution.py:311
  9.3 3.8 %collective-permute-done.1.right_ref = f32[7,64,128]{2,1,0:T(8,128)S(1)} collective-permute-done((f32[7,64,128]{2,1,0:T(8,128)S(1)}, f32[7,64,128]{2,1,0:T(8,128)S(1)}, u32[]{:S(2)}, u32[]{:S(2)}) %collective-permute-start.1) | collective-permute-done | bytes 229408 | tf_op jit(solution)/shard_map/ppermute | solution.py:312
  13.1 0.7 copy-done.2
  13.8 5.0 %shard_map.73 = f32[8,64,896]{2,1,0:T(8,128)} custom-call(f32[49,64,128]{2,1,0:T(8,128)} %bitcast.21, f32[7,64,128]{2,1,0:T(8,128)} %copy-done.1, f32[7,64,128]{2,1,0:T(8,128)} %copy-done.2, bf16[2,49,64,128]{3,2,1,0:T(8,128)(2,1)} %bitcast.24), custom_call_target="tpu_custom_call" | custom-call | tf_op jit(solution)/shard_map/pallas_call | solution.py:315
  18.8 30.9 %all_to_all.20 = f32[8,64,896]{2,1,0:T(8,128)} all-to-all(f32[8,64,896]{2,1,0:T(8,128)} %shard_map.73), channel_id=1, replica_groups=mesh['mesh'=16,'span'=8] {'span'}, dimensions={0} | all-to-all | bytes 3670016 | tf_op jit(solution)/shard_map/all_to_all | solution.py:318
  49.7 4.3 %shard_map.74 = f32[3072,128]{1,0:T(8,128)} custom-call(f32[512,896]{1,0:T(8,128)} %bitcast.13, bf16[384,512]{1,0:T(8,128)(2,1)} %constant.37.clone.high_ref, bf16[384,512]{1,0:T(8,128)(2,1)} %constant.38.clone.low_ref), custom_call_target="tpu_custom_call" | custom-call | tf_op jit(solution)/shard_map/pallas_call | solution.py:322
  54.0 9.7 %all-to-all-start.1 = ((f32[128,24,128]{2,1,0:T(8,128)}), f32[128,24,128]{2,1,0:T(8,128)S(1)}, u32[]{:S(2)}, u32[]{:S(2)}) async-start(f32[128,24,128]{2,1,0:T(8,128)} %bitcast.17), calls=%async_computation.1 | async-start | bytes 3145728 | tf_op jit(solution)/shard_map/all_to_all | solution.py:325
  63.7 0.0 copy-done.3
  63.7 32.3 %all-gather = f32[49,2048]{1,0:T(8,128)S(1)} all-gather(f32[49,128]{1,0:T(8,128)S(1)} %copy-done.3), channel_id=2, replica_groups=mesh['mesh'=16,'span'=8] {'mesh'}, dimensions={1}, use_global_device_ids=true | all-gather | bytes 426496 | tf_op jit(solution)/shard_map/all_gather | solution.py:313
  96.0 0.1 copy.10
  96.1 0.8 slice.15.damp_ref
  96.8 0.6 compare_select_fusion.1
  97.4 0.0 all-to-all-done.1
  97.4 1.1 copy-done
  98.6 23.7 %shard_map.75 = f32[3072,128]{1,0:T(8,128)} custom-call(f32[3]{0:T(128)} %get-tuple-element.8.shift_ref, f32[3]{0:T(128)} %get-tuple-element.7.idle_ref, f32[3072,128]{1,0:T(8,128)} %bitcast.16, f32[49,16,128]{2,1,0:T(8,128)} %slice.15.damp_ref), custom_call_target="tpu_custom_call" | custom-call | tf_op jit(solution)/shard_map/pallas_call | solution.py:335
  122.3 37.0 %all_to_all.21 = f32[128,24,128]{2,1,0:T(8,128)} all-to-all(f32[128,24,128]{2,1,0:T(8,128)} %bitcast.18), channel_id=1, replica_groups=mesh['mesh'=16,'span'=8] {'mesh','span'}, dimensions={0} | all-to-all | bytes 3145728 | tf_op jit(solution)/shard_map/all_to_all | solution.py:339
  159.2 4.6 %shard_map.76 = f32[512,896]{1,0:T(8,128)} custom-call(f32[3072,128]{1,0:T(8,128)} %bitcast.19, bf16[512,384]{1,0:T(8,128)(2,1)} %constant.39.clone.high_ref, bf16[512,384]{1,0:T(8,128)(2,1)} %constant.40.clone.low_ref), custom_call_target="tpu_custom_call" | custom-call | tf_op jit(solution)/shard_map/pallas_call | solution.py:342
  163.8 28.4 %all_to_all.22 = f32[8,64,896]{2,1,0:T(8,128)S(1)} all-to-all(f32[8,64,896]{2,1,0:T(8,128)} %bitcast.14), channel_id=1, replica_groups=mesh['mesh'=16,'span'=8] {'span'}, dimensions={0} | all-to-all | bytes 3670016 | tf_op jit(solution)/shard_map/all_to_all | solution.py:345
  192.2 0.1 slice.14
  192.3 0.2 reshape.30
  192.5 1.4 copy.9
  (5 shorter events, 0.0 us)
Async XLA Ops:
  1.1 8.2 %collective-permute-start = (f32[7,64,128]{2,1,0:T(8,128)S(1)}, f32[7,64,128]{2,1,0:T(8,128)S(1)}, u32[]{:S(2)}, u32[]{:S(2)}) collective-permute-start(f32[7,64,128]{2,1,0:T(8,128)S(1)} %get-tuple-element.6), channel_id=1, source_target_pairs={{0,8},{8,16},{16,24},{24,32},{32,40},{40,48},{48,56},{56,64},{64,7... | collective-permute-start | bytes 688136 | tf_op jit(solution)/shard_map/ppermute | solution.py:311
  5.0 8.0 %collective-permute-start.1 = (f32[7,64,128]{2,1,0:T(8,128)S(1)}, f32[7,64,128]{2,1,0:T(8,128)S(1)}, u32[]{:S(2)}, u32[]{:S(2)}) collective-permute-start(f32[7,64,128]{2,1,0:T(8,128)S(1)} %get-tuple-element.5), channel_id=1, source_target_pairs={{8,0},{16,8},{24,16},{32,24},{40,32},{48,40},{56,48},{64,56},{72,6... | collective-permute-start | bytes 688136 | tf_op jit(solution)/shard_map/ppermute | solution.py:312
  9.3 3.8 %copy-start.1 = (f32[7,64,128]{2,1,0:T(8,128)}, f32[7,64,128]{2,1,0:T(8,128)S(1)}, u32[]{:S(2)}) copy-start(f32[7,64,128]{2,1,0:T(8,128)S(1)} %collective-permute-done.left_ref) | copy-start | bytes 688132
  13.1 0.7 copy-start.2
  54.0 9.7 %copy-start.3 = (f32[49,128]{1,0:T(8,128)S(1)}, f32[49,128]{1,0:T(8,128)}, u32[]{:S(2)}) copy-start(f32[49,128]{1,0:T(8,128)} %param.9) | copy-start | bytes 75268
  54.0 43.4 %all-to-all-start.1 = ((f32[128,24,128]{2,1,0:T(8,128)}), f32[128,24,128]{2,1,0:T(8,128)S(1)}, u32[]{:S(2)}, u32[]{:S(2)}) async-start(f32[128,24,128]{2,1,0:T(8,128)} %bitcast.17), calls=%async_computation.1 | async-start | bytes 3145728 | tf_op jit(solution)/shard_map/all_to_all | solution.py:325
  97.4 1.1 copy-start

commit v2 on v1

v2 whole, which is shorter than its diff:
```python
import math

import jax
import jax.numpy as jnp
import ml_dtypes
import numpy as np
from jax import lax
from jax.experimental import pallas as pl
from jax.experimental.pallas import tpu as pltpu
from jax.sharding import Mesh, PartitionSpec as P

ORDER = 6
SIDE = 7
NODES = 49
EY = 128
COLS = 16
PLANES = 512
PL_DEV = 64
N_SPAN = 8
N_DEV = 128
WAVES = 168
KEPT = 336
M_DEV = 3
M_ALL = N_DEV * M_DEV
GROUPS = 6
PIECE = 16
ROWS = GROUPS * PL_DEV + 8
PAIR = GROUPS * M_DEV + 1
PADDED = 56
ITERS = 8

LAMBDA0 = 0.1
VISCOSITY = 0.02
PENALTY = 100.0
BETA = 0.02
VMEM = 16 * 1024 * 1024


def gll_tables(degree):
    side_nodes = degree + 1
    points = [-math.cos(math.pi * n / degree) for n in range(side_nodes)]
    values = [1.0] * side_nodes
    for _ in range(60):
        updated = []
        new_values = []
        for point in points:
            lower = 1.0
            now = point
            for step in range(2, degree + 1):
                lower, now = now, ((2 * step - 1) * point * now - (step - 1) * lower) / step
            updated.append(point - (point * now - lower) / (side_nodes * now))
            new_values.append(now)
        points = updated
        values = new_values
    weights = np.array([2.0 / (degree * side_nodes * v * v) for v in values])
    derivative = np.zeros((side_nodes, side_nodes))
    for row in range(side_nodes):
        for col in range(side_nodes):
            if row != col:
                derivative[row, col] = values[row] / (values[col] * (points[row] - points[col]))
    derivative[0, 0] = -degree * side_nodes / 4.0
    derivative[degree, degree] = degree * side_nodes / 4.0
    return weights, derivative


W, D = gll_tables(ORDER)
EDGE = 1.0 / (2.0 * W[0] * VISCOSITY)


def fourier_table():
    row = np.arange(M_ALL)[:, None]
    c = row % N_DEV * M_DEV + row // N_DEV
    p = np.arange(PLANES)[None, :]
    k = np.where(c < WAVES, c, c - WAVES + 1)
    phases = ((k * p) % PLANES) * (2.0 * math.pi / PLANES)
    table = np.where(c < WAVES, np.cos(phases), np.sin(phases))
    scale = np.where(c == 0, 1.0 / PLANES, 2.0 / PLANES)
    table = np.where(c < KEPT, table, 0.0)
    return table * scale, table.T


def in_two(table):
    table = table.astype(np.float32)
    high = table.astype(ml_dtypes.bfloat16)
    low = (table - high.astype(np.float32)).astype(ml_dtypes.bfloat16)
    return jnp.asarray(high), jnp.asarray(low)


def split(x):
    high = x.astype(jnp.bfloat16)
    low = (x - high.astype(jnp.float32)).astype(jnp.bfloat16)
    return high, low


def dot(a, b):
    return jnp.dot(a, b, preferred_element_type=jnp.float32)


def combine(coefs, values):
    total = None
    for c, v in zip(coefs, values):
        if c == 0.0:
            continue
        term = v * np.float32(c)
        total = term if total is None else total + term
    return total


def turn(x, by):
    by = by % EY
    return pltpu.roll(x, by, 1) if by else x


def piece_of(shape):
    return lax.broadcasted_iota(jnp.int32, shape, 1) // PIECE


def pack(blocks, turns):
    piece = piece_of(blocks[0].shape)
    out = turn(blocks[0], turns[0])
    for h in range(1, len(blocks)):
        out = jnp.where(piece == h, turn(blocks[h], turns[h]), out)
    return out


def inner_kernel(q_ref, a_ref, out_ref):
    table = D / VISCOSITY
    own = table.copy()
    own[6, 6] -= EDGE
    own[0, 0] += EDGE
    edge = np.float32(EDGE)

    def block(b, carry):
        rows = pl.ds(pl.multiple_of(b * 16, 16), 16)
        for i in range(SIDE):
            line = [q_ref[i * SIDE + j, rows, :] for j in range(SIDE)]
            gy = [combine(own[j], line) for j in range(SIDE)]
            gy[6] = gy[6] + edge * pltpu.roll(line[0], EY - 1, 1)
            gy[0] = gy[0] - edge * pltpu.roll(line[6], 1, 1)
            for j in range(SIDE):
                n = i * SIDE + j
                gx = combine(own[i], [q_ref[a * SIDE + j, rows, :] for a in range(SIDE)])
                ax = a_ref[0, n, rows, :].astype(jnp.float32)
                ay = a_ref[1, n, rows, :].astype(jnp.float32)
                out_ref[n, rows, :] = np.float32(LAMBDA0) * line[j] - (ax * gx + ay * gy[j])
        return carry

    lax.fori_loop(0, PL_DEV // 16, block, 0)


def outer_kernel(
    place_ref, inner_ref, left_ref, right_ref, across_ref, damp_ref, a_ref, out_ref, row_ref, last_ref
):
    column = place_ref[0]
    has_left = jnp.where(column > 0, 1.0, 0.0)
    has_right = jnp.where(column < COLS - 1, 1.0, 0.0)
    edge = np.float32(EDGE)
    for n in range(NODES):
        target = last_ref if n == NODES - 1 else out_ref.at[n // GROUPS]
        start = 0 if n == NODES - 1 else n % GROUPS * PL_DEV
        j = n % SIDE
        face = slice(j * PL_DEV, (j + 1) * PL_DEV)
        value = inner_ref[n]
        if n < SIDE:
            value = value + (edge * has_left) * left_ref[face, :] * a_ref[0, n].astype(jnp.float32)
        if n >= NODES - SIDE:
            value = value - (edge * has_right) * right_ref[face, :] * a_ref[0, n].astype(jnp.float32)
        target[start : start + PL_DEV, :] = value
    for s in range(N_SPAN):
        blocks = [last_ref[8 * h : 8 * h + 8, :] for h in range(8)]
        out_ref[s, GROUPS * PL_DEV :, :] = pack(blocks, [PIECE * (h - s) for h in range(8)])
    x = lax.rem(column, 4)
    row_ref[...] = jnp.zeros(row_ref.shape, jnp.float32)
    faces = SIDE * PL_DEV
    for step, rows in ((0, damp_ref[...]), (1, right_ref[faces:, :]), (2, across_ref[...]), (3, left_ref[faces:, :])):
        row_ref[pl.ds(pl.multiple_of(lax.rem(x + step, 4) * PADDED, 8), NODES), :] = rows[:NODES]


def product(table_refs, x):
    high, low = table_refs
    xh, xl = split(x)
    return dot(high[...], xh) + (dot(high[...], xl) + dot(low[...], xh))


def forward_kernel(x_ref, high_ref, low_ref, out_ref):
    table = (high_ref, low_ref)
    for start in range(0, GROUPS, 2):
        x = jnp.concatenate(
            [
                jnp.concatenate([x_ref[s, g * PL_DEV : (g + 1) * PL_DEV, :] for s in range(N_SPAN)], axis=0)
                for g in (start, start + 1)
            ],
            axis=1,
        )
        res = product(table, x)
        for g in range(2):
            for j in range(M_DEV):
                out_ref[pl.ds(j * GROUPS + start + g, N_DEV, stride=PAIR), :] = res[
                    j * N_DEV : (j + 1) * N_DEV, g * EY : (g + 1) * EY
                ]
    packed = [x_ref[s, GROUPS * PL_DEV :, :] for s in range(N_SPAN)]
    x = jnp.concatenate([turn(packed[s], -PIECE * h) for s in range(N_SPAN) for h in range(8)], axis=0)
    res = product(table, x)
    parts = [res[j * N_DEV : (j + 1) * N_DEV] for j in range(M_DEV)]
    out_ref[pl.ds(PAIR - 1, N_DEV, stride=PAIR), :] = pack(parts, [PIECE * j for j in range(M_DEV)])


def inverse_kernel(x_ref, high_ref, low_ref, out_ref):
    table = (high_ref, low_ref)
    for start in range(0, GROUPS, 2):
        x = jnp.concatenate(
            [
                jnp.concatenate(
                    [x_ref[pl.ds(j * GROUPS + g, N_DEV, stride=PAIR), :] for j in range(M_DEV)], axis=0
                )
                for g in (start, start + 1)
            ],
            axis=1,
        )
        res = product(table, x)
        for g in range(2):
            for s in range(N_SPAN):
                out_ref[s, (start + g) * PL_DEV : (start + g + 1) * PL_DEV, :] = res[
                    s * PL_DEV : (s + 1) * PL_DEV, g * EY : (g + 1) * EY
                ]
    rest = x_ref[pl.ds(PAIR - 1, N_DEV, stride=PAIR), :]
    x = jnp.concatenate([turn(rest, -PIECE * j) for j in range(M_DEV)], axis=0)
    res = product(table, x)
    for s in range(N_SPAN):
        blocks = [res[s * PL_DEV + 8 * h : s * PL_DEV + 8 * h + 8] for h in range(8)]
        out_ref[s, GROUPS * PL_DEV :, :] = pack(blocks, [PIECE * h for h in range(8)])


def final_kernel(x_ref, out_ref):
    for s in range(N_SPAN):
        for g in range(GROUPS):
            out_ref[s * GROUPS + g] = x_ref[s, g * PL_DEV : (g + 1) * PL_DEV, :]
    packed = [x_ref[s, GROUPS * PL_DEV :, :] for s in range(N_SPAN)]
    for h in range(8):
        out_ref[NODES - 1, 8 * h : 8 * h + 8, :] = pack(packed, [PIECE * (s - h) for s in range(N_SPAN)])


def solve_tables():
    own = D.T @ np.diag(W) @ D
    own[6, 6] += PENALTY
    own[6, :] -= D[6, :] / 2
    own[:, 6] -= D[6, :] / 2
    own[0, 0] += PENALTY
    own[0, :] += D[0, :] / 2
    own[:, 0] += D[0, :] / 2
    return own


OWN = solve_tables()


def line_image(v, weight, from_next, from_before):
    own, d6, penalty = OWN * weight, D[6] * weight, np.float32(PENALTY * weight)
    even = [v[0] + v[6], v[1] + v[5], v[2] + v[4], v[3]]
    odd = [v[0] - v[6], v[1] - v[5], v[2] - v[4]]
    d_even = [(d6[a] + d6[6 - a]) / 2 for a in range(3)] + [d6[3]]
    d_odd = [(d6[a] - d6[6 - a]) / 2 for a in range(3)]
    half_even = combine([c / 2 for c in d_even], even)
    half_odd = combine([c / 2 for c in d_odd], odd)
    first = penalty * v[0] + (half_odd - half_even)
    last = penalty * v[6] - (half_even + half_odd)
    next_value = from_next(v[0])
    next_first = from_next(first)
    before_value = from_before(v[6])
    before_last = from_before(last)
    sum_value = next_value + before_value
    dif_value = next_value - before_value
    out = [None] * SIDE
    for i in range(3):
        e = combine(
            [(own[i, a] + own[i, 6 - a]) / 2 for a in range(3)] + [own[i, 3], d_even[i] / 2],
            even + [sum_value],
        )
        o = combine(
            [(own[i, a] - own[i, 6 - a]) / 2 for a in range(3)] + [d_odd[i] / 2],
            odd + [dif_value],
        )
        out[i] = e + o
        out[6 - i] = e - o
    out[3] = combine([own[3, a] for a in range(4)] + [d6[3] / 2], even + [sum_value])
    out[6] = out[6] - next_first
    out[0] = out[0] - before_last
    return out


def whole_sum(x):
    return jnp.sum(jnp.sum(x, axis=0, keepdims=True), axis=1, keepdims=True)


def solve_kernel(
    shift_ref, idle_ref, place_ref, b_ref, damp_ref, out_ref, mass_ref, x_ref, r_ref, p_ref, q_ref, ratio_ref, part_ref
):
    stride = N_SPAN * PAIR
    piece = piece_of((COLS, EY))
    half = COLS // 2
    column = lax.broadcasted_iota(jnp.int32, (half, EY), 0)
    zero = jnp.zeros((COLS, EY), jnp.float32)

    def load(ref, start, step):
        return jnp.concatenate(
            [ref[pl.ds(start, half, stride=2 * step), :], ref[pl.ds(start + step, half, stride=2 * step), :]],
            axis=0,
        )

    def store(start, step, value):
        out_ref[pl.ds(start, half, stride=2 * step), :] = value[:half]
        out_ref[pl.ds(start + step, half, stride=2 * step), :] = value[half:]

    def x_next(v):
        return jnp.concatenate(
            [v[half:], jnp.where(column < half - 1, pltpu.roll(v[:half], half - 1, 0), 0.0)], axis=0
        )

    def x_before(v):
        return jnp.concatenate([jnp.where(column > 0, pltpu.roll(v[half:], 1, 0), 0.0), v[:half]], axis=0)

    def y_next(v):
        return pltpu.roll(v, EY - 1, 1)

    def y_before(v):
        return pltpu.roll(v, 1, 1)

    def totals():
        return [whole_sum(part_ref[mode]) for mode in range(M_DEV)]

    place = lax.rem(place_ref[0], 4)
    wrap_odd = jnp.logical_and(place == 0, column % 2 == 1)
    wrap_even = jnp.logical_and(place == 3, column % 2 == 0)

    def damp_of(n):
        even = damp_ref[pl.ds(n, half, stride=2 * PADDED), :]
        odd = damp_ref[pl.ds(n + PADDED, half, stride=2 * PADDED), :]
        even = jnp.where(wrap_even, pltpu.roll(even, 2, 0), even)
        odd = jnp.where(wrap_odd, pltpu.roll(odd, half - 2, 0), odd)
        return jnp.concatenate([even, odd], axis=0)

    def begin(mode, carry):
        shift = shift_ref[mode]
        base = mode * NODES
        norm = zero
        for n in range(NODES):
            w = np.float32(W[n // SIDE] * W[n % SIDE])
            if n < NODES - 1:
                start = n // GROUPS * PAIR + n % GROUPS
                rows = load(b_ref, start + mode * GROUPS, stride)
            else:
                rows = zero
                for s in range(N_SPAN):
                    rest = load(b_ref, s * PAIR + PAIR - 1, stride)
                    own = pltpu.roll(rest, lax.rem(s * PIECE + EY - mode * PIECE, EY), 1)
                    rows = jnp.where(piece == s, own, rows)
            damp = damp_of(n)
            rhs = w * rows
            r_ref[base + n] = rhs
            p_ref[base + n] = zero
            x_ref[base + n] = zero
            mass_ref[base + n] = w * (damp + shift)
            norm = norm + rhs * rhs
        part_ref[mode] = norm
        ratio_ref[mode] = zero
        return carry

    lax.fori_loop(0, M_DEV, begin, 0)

    def apply(mode, carry):
        base = mode * NODES
        ratio = ratio_ref[mode]
        for j in range(SIDE):
            line = []
            for i in range(SIDE):
                n = base + i * SIDE + j
                p = r_ref[n] + ratio * p_ref[n]
                p_ref[n] = p
                line.append(p)
            image = line_image(line, W[j], x_next, x_before)
            for i in range(SIDE):
                n = base + i * SIDE + j
                q_ref[n] = image[i] + mass_ref[n] * line[i]
        curve = zero
        for i in range(SIDE):
            line = [p_ref[base + i * SIDE + j] for j in range(SIDE)]
            image = line_image(line, W[i], y_next, y_before)
            for j in range(SIDE):
                n = base + i * SIDE + j
                q = q_ref[n] + image[j]
                q_ref[n] = q
                curve = curve + q * line[j]
        part_ref[mode] = curve
        return carry

    def update(mode, carry):
        base = mode * NODES
        alpha = ratio_ref[mode]
        fresh = zero
        for n in range(NODES):
            x_ref[base + n] = x_ref[base + n] + alpha * p_ref[base + n]
            r = r_ref[base + n] - alpha * q_ref[base + n]
            r_ref[base + n] = r
            fresh = fresh + r * r
        part_ref[mode] = fresh
        return carry

    def spread(values):
        for mode in range(M_DEV):
            ratio_ref[mode] = jnp.broadcast_to(values[mode], (COLS, EY))

    def iteration(step, norm):
        lax.fori_loop(0, M_DEV, apply, 0)
        curve = totals()
        spread([norm[m] / (curve[m] + idle_ref[m]) for m in range(M_DEV)])
        lax.fori_loop(0, M_DEV, update, 0)
        fresh = totals()
        spread([fresh[m] / (norm[m] + idle_ref[m]) for m in range(M_DEV)])
        return tuple(fresh)

    lax.fori_loop(0, ITERS, iteration, tuple(totals()))

    def finish(mode, carry):
        base = mode * NODES
        for n in range(NODES - 1):
            start = n // GROUPS * PAIR + n % GROUPS
            store(start + mode * GROUPS, stride, x_ref[base + n])
        return carry

    lax.fori_loop(0, M_DEV, finish, 0)
    for s in range(N_SPAN):
        own = zero
        for mode in range(M_DEV):
            rest = turn(x_ref[mode * NODES + NODES - 1], (mode - s) * PIECE)
            own = jnp.where(piece == mode, rest, own)
        store(s * PAIR + PAIR - 1, stride, own)


def f32(shape):
    return jax.ShapeDtypeStruct(shape, jnp.float32)


def call(kernel, shape, scratch=(), smem=0, n_in=0):
    full = pl.BlockSpec(memory_space=pltpu.VMEM)
    scalar = pl.BlockSpec(memory_space=pltpu.SMEM)
    many = isinstance(shape, list)
    return pl.pallas_call(
        kernel,
        out_shape=[f32(s) for s in shape] if many else f32(shape),
        in_specs=[scalar] * smem + [full] * n_in,
        out_specs=[full] * len(shape) if many else full,
        scratch_shapes=[pltpu.VMEM(s, jnp.float32) for s in scratch],
        compiler_params=pltpu.CompilerParams(vmem_limit_bytes=VMEM),
    )


def body(velocity_q, advecting, damping):
    columns = ("y", "x")
    span = ("z", "core")
    everyone = columns + span
    up = [(i, (i + 1) % COLS) for i in range(COLS)]
    down = [(j, i) for i, j in up]
    q_nodes = jnp.transpose(velocity_q, (1, 0, 2))
    a_nodes = jnp.transpose(advecting, (0, 2, 1, 3))
    blank = jnp.zeros((PADDED - NODES, EY), jnp.float32)

    def beside(face):
        return jnp.concatenate([face.reshape(SIDE * PL_DEV, EY), damping, blank])

    from_left = lax.ppermute(beside(q_nodes[NODES - SIDE :]), columns, up)
    from_right = lax.ppermute(beside(q_nodes[:SIDE]), columns, down)
    across = lax.ppermute(damping, "x", [(i, (i + 2) % 4) for i in range(4)])
    inner = call(inner_kernel, (NODES, PL_DEV, EY), n_in=2)(q_nodes, a_nodes)
    place = lax.axis_index(columns).astype(jnp.int32)[None]
    forcing, damp_row = call(
        outer_kernel, [(N_SPAN, ROWS, EY), (4 * PADDED, EY)], scratch=((PL_DEV, EY),), smem=1, n_in=6
    )(place, inner, from_left, from_right, across, damping, a_nodes)
    device = lax.axis_index(everyone)
    coef = device * M_DEV + jnp.arange(M_DEV, dtype=jnp.int32)
    wave = jnp.where(coef < WAVES, coef, coef - WAVES + 1).astype(jnp.float32)
    shifts = LAMBDA0 + (BETA * wave) ** 2
    idle = jnp.where(coef < KEPT, 0.0, 1.0).astype(jnp.float32)
    forcing, damp_row, shifts, idle = lax.optimization_barrier((forcing, damp_row, shifts, idle))
    planes = lax.all_to_all(forcing, span, split_axis=0, concat_axis=0, tiled=True)
    damp_nodes = lax.all_gather(damp_row, "y", axis=0, tiled=True)
    planes, damp_nodes = lax.optimization_barrier((planes, damp_nodes))

    forward, backward = fourier_table()
    spectra = call(forward_kernel, (N_DEV * PAIR, EY), n_in=3)(planes, *in_two(forward))
    mine = lax.all_to_all(
        spectra.reshape(N_DEV, 1, PAIR * EY), everyone, split_axis=0, concat_axis=0, tiled=True
    )

    field, part = (M_DEV * NODES, COLS, EY), (M_DEV, COLS, EY)
    solved = call(solve_kernel, (N_DEV * PAIR, EY), scratch=(field,) * 5 + (part,) * 2, smem=3, n_in=2)(
        shifts, idle, place, mine.reshape(N_DEV * PAIR, EY), damp_nodes
    )

    modes = lax.all_to_all(
        solved.reshape(N_DEV, 1, PAIR * EY), everyone, split_axis=0, concat_axis=0, tiled=True
    )
    physical = call(inverse_kernel, (N_SPAN, ROWS, EY), n_in=3)(
        modes.reshape(N_DEV * PAIR, EY), *in_two(backward)
    )
    back = lax.all_to_all(physical, span, split_axis=0, concat_axis=0, tiled=True)
    q_new = call(final_kernel, (NODES, PL_DEV, EY), n_in=1)(back)
    return jnp.transpose(q_new, (1, 0, 2))


def solution(mesh):
    columns, span = ("y", "x"), ("z", "core")
    side = math.isqrt(COLS)
    parts = Mesh(mesh.devices.reshape(side, side, N_SPAN // 2, 2), columns + span)
    placed = (P(span, None, columns), P(None, span, None, columns), P(None, columns))
    return jax.shard_map(
        body, mesh=parts, in_specs=placed, out_specs=P(span, None, columns), check_vma=False
    )
```

time: 195 us -> 148 us (0.76)
  blocking collectives: 128 us -> 86.6 us
  Pallas kernels: 37.6 us -> 26.3 us
  waiting for transfers between devices: 6.75 us -> 18 us
  local copies, waits for them, and re-layouts: 5.56 us -> 2.72 us
  starting transfers between devices: 14.9 us -> 12.9 us
    all_gather x1, blocking collectives: 32.3 us -> 10.9 us  [body(): damp_nodes = lax.all_gather(damp_row, 'y', axis=0, tiled=True)]
    all_to_all x3, blocking collectives: 96.2 us -> 75.7 us  [the longest x1 25.5 us: body(): lax.all_to_all(solved.reshape(N_DEV, 1, PAIR * EY), everyone, split_axis=...]
    pallas_call x4 -> x6, Pallas kernels: 37.6 us -> 26.3 us  [the longest x1 18.8 us: body(): call(solve_kernel, (N_DEV * PAIR, EY), scratch=(field,) * 5 + (part,) * 2...]
    all_to_all x1, waiting for transfers between devices: 0.01 us -> 10.2 us  [body(): lax.all_to_all(forcing, span, split_axis=0, concat_axis=0, tiled=True)]
    all_to_all x1, starting transfers between devices: 9.68 us -> 7.1 us  [body(): lax.all_to_all(forcing, span, split_axis=0, concat_axis=0, tiled=True)]
    ppermute x2 -> x3, waiting for transfers between devices: 6.74 us -> 7.8 us  [the longest x1 5.4 us: body(): from_left = lax.ppermute(beside(q_nodes[NODES - SIDE:]), columns, up)]
    ppermute x2 -> x3, starting transfers between devices: 5.25 us -> 5.83 us  [the longest x1 5.83 us: body(): from_right = lax.ppermute(beside(q_nodes[:SIDE]), columns, down)]
  transfers between devices with their start and end apart: 3 -> 4, of which waited for: 2 -> 3; matrix products, arithmetic and copies ran while one was open for 1% -> 0% of each run, Pallas kernels for 0% -> 1%
where the time goes in v2:
time: 148 us
  blocking collectives  86.6 us (59%)
  Pallas kernels  26.3 us (18%)
  waiting for transfers between devices  18 us (12%)
  starting transfers between devices  12.9 us (9%)
  local copies, waits for them, and re-layouts  2.72 us (2%)
    all_to_all x1, blocking collectives, body(): lax.all_to_all(solved.reshape(N_DEV, 1, PAIR * EY), everyone, split_axis=...  25.5 us
    all_to_all x1, blocking collectives, body(): lax.all_to_all(physical, span, split_axis=0, concat_axis=0, tiled=True)  25.2 us
    all_to_all x1, blocking collectives, body(): lax.all_to_all(spectra.reshape(N_DEV, 1, PAIR * EY), everyone, split_axis...  25 us
    pallas_call x1, Pallas kernels, body(): call(solve_kernel, (N_DEV * PAIR, EY), scratch=(field,) * 5 + (part,) * 2...  18.8 us
    all_gather x1, blocking collectives, body(): damp_nodes = lax.all_gather(damp_row, 'y', axis=0, tiled=True)  10.9 us
    all_to_all x1, waiting for transfers between devices, body(): lax.all_to_all(forcing, span, split_axis=0, concat_axis=0, tiled=True)  10.2 us
    all_to_all x1, starting transfers between devices, body(): lax.all_to_all(forcing, span, split_axis=0, concat_axis=0, tiled=True)  7.1 us
    ppermute x1, starting transfers between devices, body(): from_right = lax.ppermute(beside(q_nodes[:SIDE]), columns, down)  5.83 us
  transfers between devices with their start and end apart: 4, of which 3 were waited for; matrix products, arithmetic and copies ran while one was open for 0% of the time, Pallas kernels for 1%

profile of v2, /device:TPU:1, one launch (start us, length us, event | category | flops | bytes accessed | tf_op | source)
XLA Modules:
  0.0 147.5 jit_solution(2430233628785213049)
XLA Ops:
  0.0 1.2 fusion.6
  1.2 0.1 pad.5.clone
  1.3 0.9 fusion.1
  2.2 5.8 %collective-permute-start.1 = (f32[504,128]{1,0:T(8,128)S(1)}, f32[504,128]{1,0:T(8,128)S(1)}, u32[]{:S(2)}, u32[]{:S(2)}) collective-permute-start(f32[504,128]{1,0:T(8,128)S(1)} %get-tuple-element.23), channel_id=1, source_target_pairs={{8,0},{16,8},{24,16},{32,24},{40,32},{48,40},{56,48},{64,56},{72,6... | collective-permute-start | bytes 774152 | tf_op jit(solution)/shard_map/ppermute | solution.py:471
  8.0 0.0 collective-permute-start
  8.0 0.0 collective-permute-start.2
  8.1 0.0 copy-start.1
  8.1 1.4 copy-done.1
  9.5 1.6 %shard_map.73.inner_ref = f32[49,64,128]{2,1,0:T(8,128)S(1)} custom-call(f32[49,64,128]{2,1,0:T(8,128)S(1)} %bitcast.17, bf16[2,49,64,128]{3,2,1,0:T(8,128)(2,1)S(1)} %bitcast.10), custom_call_target="tpu_custom_call" | custom-call | tf_op jit(solution)/shard_map/pallas_call | solution.py:473
  11.1 2.4 %collective-permute-done.2.across_ref = f32[49,128]{1,0:T(8,128)S(1)} collective-permute-done((f32[49,128]{1,0:T(8,128)S(1)}, f32[49,128]{1,0:T(8,128)S(1)}, u32[]{:S(2)}, u32[]{:S(2)}) %collective-permute-start.2) | collective-permute-done | bytes 25120 | tf_op jit(solution)/shard_map/ppermute | solution.py:472
  13.5 5.4 %collective-permute-done.left_ref = f32[504,128]{1,0:T(8,128)S(1)} collective-permute-done((f32[504,128]{1,0:T(8,128)S(1)}, f32[504,128]{1,0:T(8,128)S(1)}, u32[]{:S(2)}, u32[]{:S(2)}) %collective-permute-start) | collective-permute-done | bytes 258080 | tf_op jit(solution)/shard_map/ppermute | solution.py:470
  18.9 1.4 shard_map.74
  20.3 7.1 %all-to-all-start = ((f32[8,392,128]{2,1,0:T(8,128)}), f32[8,392,128]{2,1,0:T(8,128)S(1)}, u32[]{:S(2)}, u32[]{:S(2)}) async-start(f32[8,392,128]{2,1,0:T(8,128)} %get-tuple-element.17), calls=%async_computation | async-start | bytes 3211264 | tf_op jit(solution)/shard_map/all_to_all | solution.py:484
  27.4 10.9 %all_gather.3.damp_ref = f32[896,128]{1,0:T(8,128)S(1)} all-gather(f32[224,128]{1,0:T(8,128)S(1)} %get-tuple-element.18), channel_id=1, replica_groups=mesh['y'=4,'x'=4,'z'=4,'core'=2] {'y'}, dimensions={0}, use_global_device_ids=true | all-gather | bytes 573440 | tf_op jit(solution)/shard_map/all_gather | solution.py:485
  38.2 10.2 %all-to-all-done.x_ref = f32[8,392,128]{2,1,0:T(8,128)S(1)} async-done(((f32[8,392,128]{2,1,0:T(8,128)}), f32[8,392,128]{2,1,0:T(8,128)S(1)}, u32[]{:S(2)}, u32[]{:S(2)}) %all-to-all-start) | async-done | bytes 1605664 | tf_op jit(solution)/shard_map/all_to_all | solution.py:484
  48.4 1.5 shard_map.75
  49.9 25.0 %all_to_all.20 = f32[128,1,2432]{2,1,0:T(1,128)S(1)} all-to-all(f32[128,1,2432]{2,1,0:T(1,128)S(1)} %bitcast.14), channel_id=1, replica_groups=mesh['y'=4,'x'=4,'z'=4,'core'=2] {'y','x','z','core'}, dimensions={0} | all-to-all | bytes 2490368 | tf_op jit(solution)/shard_map/all_to_all | solution.py:490
  74.9 18.8 %shard_map.76 = f32[2432,128]{1,0:T(8,128)S(1)} custom-call(f32[3]{0:T(128)S(1)} %get-tuple-element.15.shift_ref, f32[3]{0:T(128)S(1)} %get-tuple-element.16.idle_ref, s32[1]{0:T(128)} %bitcast.place_ref, f32[2432,128]{1,0:T(8,128)S(1)} %bitcast.12, f32[896,128]{1,0:T(8,128)S(1)} %all_gather.3.damp_ref), custom_call_target="tpu_custom_call" | custom-call | tf_op jit(solution)/shard_map/pallas_call | solution.py:495
  93.8 0.0 copy-start.2
  93.8 0.0 copy-start.3
  93.8 25.5 %all_to_all.21 = f32[128,1,2432]{2,1,0:T(1,128)S(1)} all-to-all(f32[128,1,2432]{2,1,0:T(1,128)S(1)} %bitcast.13), channel_id=1, replica_groups=mesh['y'=4,'x'=4,'z'=4,'core'=2] {'y','x','z','core'}, dimensions={0} | all-to-all | bytes 2490368 | tf_op jit(solution)/shard_map/all_to_all | solution.py:499
  119.3 1.8 %shard_map.77 = f32[8,392,128]{2,1,0:T(8,128)S(1)} custom-call(f32[2432,128]{1,0:T(8,128)S(1)} %bitcast.15, bf16[512,384]{1,0:T(8,128)(2,1)S(1)} %copy-done.3, bf16[512,384]{1,0:T(8,128)(2,1)S(1)} %copy-done.2), custom_call_target="tpu_custom_call" | custom-call | tf_op jit(solution)/shard_map/pallas_call | solution.py:502
  121.1 25.2 %all_to_all.22.x_ref = f32[8,392,128]{2,1,0:T(8,128)S(1)} all-to-all(f32[8,392,128]{2,1,0:T(8,128)S(1)} %shard_map.77), channel_id=1, replica_groups=mesh['y'=4,'x'=4,'z'=4,'core'=2] {'z','core'}, dimensions={0} | all-to-all | bytes 3211264 | tf_op jit(solution)/shard_map/all_to_all | solution.py:505
  146.3 1.3 shard_map.78
  (13 shorter events, 0.0 us)
Async XLA Ops:
  0.0 8.0 %copy-start.6 = (f32[49,128]{1,0:T(8,128)S(1)}, f32[49,128]{1,0:T(8,128)}, u32[]{:S(2)}) copy-start(f32[49,128]{1,0:T(8,128)} %damp_ref.1) | copy-start | bytes 75268
  0.0 8.1 %copy-start = (bf16[2,64,49,128]{3,1,2,0:T(8,128)(2,1)S(1)}, bf16[2,64,49,128]{3,1,2,0:T(8,128)(2,1)}, u32[]{:S(2)}) copy-start(bf16[2,64,49,128]{3,1,2,0:T(8,128)(2,1)} %param.8) | copy-start | bytes 4816900
  2.2 11.3 %collective-permute-start.1 = (f32[504,128]{1,0:T(8,128)S(1)}, f32[504,128]{1,0:T(8,128)S(1)}, u32[]{:S(2)}, u32[]{:S(2)}) collective-permute-start(f32[504,128]{1,0:T(8,128)S(1)} %get-tuple-element.23), channel_id=1, source_target_pairs={{8,0},{16,8},{24,16},{32,24},{40,32},{48,40},{56,48},{64,56},{72,6... | collective-permute-start | bytes 774152 | tf_op jit(solution)/shard_map/ppermute | solution.py:471
  8.0 10.9 %collective-permute-start = (f32[504,128]{1,0:T(8,128)S(1)}, f32[504,128]{1,0:T(8,128)S(1)}, u32[]{:S(2)}, u32[]{:S(2)}) collective-permute-start(f32[504,128]{1,0:T(8,128)S(1)} %get-tuple-element.24), channel_id=1, source_target_pairs={{0,8},{8,16},{16,24},{24,32},{32,40},{40,48},{48,56},{56,64},{64,7... | collective-permute-start | bytes 774152 | tf_op jit(solution)/shard_map/ppermute | solution.py:470
  8.0 5.5 %collective-permute-start.2 = (f32[49,128]{1,0:T(8,128)S(1)}, f32[49,128]{1,0:T(8,128)S(1)}, u32[]{:S(2)}, u32[]{:S(2)}) collective-permute-start(f32[49,128]{1,0:T(8,128)S(1)} %copy-done.6), channel_id=1, source_target_pairs={{0,16},{8,24},{16,0},{24,8},{1,17},{9,25},{17,1},{25,9},{2,18},{10... | collective-permute-start | bytes 75272 | tf_op jit(solution)/shard_map/ppermute | solution.py:472
  8.1 1.4 copy-start.1
  20.3 28.2 %copy-start.4 = (bf16[384,512]{1,0:T(8,128)(2,1)S(1)}, bf16[384,512]{1,0:T(8,128)(2,1)}, u32[]{:S(2)}) copy-start(bf16[384,512]{1,0:T(8,128)(2,1)} %constant.51.clone.low_ref) | copy-start | bytes 1179652
  20.3 28.2 %copy-start.5 = (bf16[384,512]{1,0:T(8,128)(2,1)S(1)}, bf16[384,512]{1,0:T(8,128)(2,1)}, u32[]{:S(2)}) copy-start(bf16[384,512]{1,0:T(8,128)(2,1)} %constant.50.clone.high_ref) | copy-start | bytes 1179652
  20.3 28.2 %all-to-all-start = ((f32[8,392,128]{2,1,0:T(8,128)}), f32[8,392,128]{2,1,0:T(8,128)S(1)}, u32[]{:S(2)}, u32[]{:S(2)}) async-start(f32[8,392,128]{2,1,0:T(8,128)} %get-tuple-element.17), calls=%async_computation | async-start | bytes 3211264 | tf_op jit(solution)/shard_map/all_to_all | solution.py:484
  93.8 25.5 %copy-start.2 = (bf16[512,384]{1,0:T(8,128)(2,1)S(1)}, bf16[512,384]{1,0:T(8,128)(2,1)}, u32[]{:S(2)}) copy-start(bf16[512,384]{1,0:T(8,128)(2,1)} %constant.53.clone.low_ref) | copy-start | bytes 1179652
  93.8 25.5 %copy-start.3 = (bf16[512,384]{1,0:T(8,128)(2,1)S(1)}, bf16[512,384]{1,0:T(8,128)(2,1)}, u32[]{:S(2)}) copy-start(bf16[512,384]{1,0:T(8,128)(2,1)} %constant.52.clone.high_ref) | copy-start | bytes 1179652

commit v3 on v2

--- a/solution.py
+++ b/solution.py
@@ -288,6 +288,10 @@
     return out
 
 
+def first_row(s):
+    return (s % 2 * (N_SPAN // 2) + s // 2) * COLS * PAIR
+
+
 def whole_sum(x):
     return jnp.sum(jnp.sum(x, axis=0, keepdims=True), axis=1, keepdims=True)
 
@@ -295,7 +299,7 @@
 def solve_kernel(
     shift_ref, idle_ref, place_ref, b_ref, damp_ref, out_ref, mass_ref, x_ref, r_ref, p_ref, q_ref, ratio_ref, part_ref
 ):
-    stride = N_SPAN * PAIR
+    stride = PAIR
     piece = piece_of((COLS, EY))
     half = COLS // 2
     column = lax.broadcasted_iota(jnp.int32, (half, EY), 0)
@@ -346,12 +350,12 @@
         for n in range(NODES):
             w = np.float32(W[n // SIDE] * W[n % SIDE])
             if n < NODES - 1:
-                start = n // GROUPS * PAIR + n % GROUPS
+                start = first_row(n // GROUPS) + n % GROUPS
                 rows = load(b_ref, start + mode * GROUPS, stride)
             else:
                 rows = zero
                 for s in range(N_SPAN):
-                    rest = load(b_ref, s * PAIR + PAIR - 1, stride)
+                    rest = load(b_ref, first_row(s) + PAIR - 1, stride)
                     own = pltpu.roll(rest, lax.rem(s * PIECE + EY - mode * PIECE, EY), 1)
                     rows = jnp.where(piece == s, own, rows)
             damp = damp_of(n)
@@ -413,7 +417,8 @@
         lax.fori_loop(0, M_DEV, apply, 0)
         curve = totals()
         spread([norm[m] / (curve[m] + idle_ref[m]) for m in range(M_DEV)])
-        lax.fori_loop(0, M_DEV, update, 0)
+        for mode in range(M_DEV):
+            update(mode, 0)
         fresh = totals()
         spread([fresh[m] / (norm[m] + idle_ref[m]) for m in range(M_DEV)])
         return tuple(fresh)
@@ -423,7 +428,7 @@
     def finish(mode, carry):
         base = mode * NODES
         for n in range(NODES - 1):
-            start = n // GROUPS * PAIR + n % GROUPS
+            start = first_row(n // GROUPS) + n % GROUPS
             store(start + mode * GROUPS, stride, x_ref[base + n])
         return carry
 
@@ -433,7 +438,7 @@
         for mode in range(M_DEV):
             rest = turn(x_ref[mode * NODES + NODES - 1], (mode - s) * PIECE)
             own = jnp.where(piece == mode, rest, own)
-        store(s * PAIR + PAIR - 1, stride, own)
+        store(first_row(s) + PAIR - 1, stride, own)
 
 
 def f32(shape):
@@ -457,7 +462,7 @@
 def body(velocity_q, advecting, damping):
     columns = ("y", "x")
     span = ("z", "core")
-    everyone = columns + span
+    everyone = ("core", "z") + columns
     up = [(i, (i + 1) % COLS) for i in range(COLS)]
     down = [(j, i) for i, j in up]
     q_nodes = jnp.transpose(velocity_q, (1, 0, 2))

time: 148 us -> 143 us (0.966)
  waiting for transfers between devices: 18 us -> 12.9 us
  blocking collectives: 86.6 us -> 89.7 us
  Pallas kernels: 26.3 us -> 24.1 us
    ppermute x1, waiting for transfers between devices: 5.4 us -> 0.92 us  [body(): from_left = lax.ppermute(beside(q_nodes[NODES - SIDE:]), columns, up)]
    all_to_all x1, blocking collectives: 25 us -> 28.1 us  [body(): lax.all_to_all(spectra.reshape(N_DEV, 1, PAIR * EY), everyone, split_axis...]
    pallas_call x1, Pallas kernels: 18.8 us -> 16.6 us  [body(): call(solve_kernel, (N_DEV * PAIR, EY), scratch=(field,) * 5 + (part,) * 2...]
    ppermute x1, starting transfers between devices: 0.01 us -> 2.11 us  [body(): from_left = lax.ppermute(beside(q_nodes[NODES - SIDE:]), columns, up)]
    ppermute x1, starting transfers between devices: 5.83 us -> 3.8 us  [body(): from_right = lax.ppermute(beside(q_nodes[:SIDE]), columns, down)]
where the time goes in v3:
time: 143 us
  blocking collectives  89.7 us (63%)
  Pallas kernels  24.1 us (17%)
  waiting for transfers between devices  12.9 us (9%)
  starting transfers between devices  12.6 us (9%)
  local copies, waits for them, and re-layouts  2.72 us (2%)
    all_to_all x1, blocking collectives, body(): lax.all_to_all(spectra.reshape(N_DEV, 1, PAIR * EY), everyone, split_axis...  28.1 us
    all_to_all x1, blocking collectives, body(): lax.all_to_all(physical, span, split_axis=0, concat_axis=0, tiled=True)  25.5 us
    all_to_all x1, blocking collectives, body(): lax.all_to_all(solved.reshape(N_DEV, 1, PAIR * EY), everyone, split_axis=...  25.3 us
    pallas_call x1, Pallas kernels, body(): call(solve_kernel, (N_DEV * PAIR, EY), scratch=(field,) * 5 + (part,) * 2...  16.6 us
    all_gather x1, blocking collectives, body(): damp_nodes = lax.all_gather(damp_row, 'y', axis=0, tiled=True)  10.9 us
    all_to_all x1, waiting for transfers between devices, body(): lax.all_to_all(forcing, span, split_axis=0, concat_axis=0, tiled=True)  10.2 us
    all_to_all x1, starting transfers between devices, body(): lax.all_to_all(forcing, span, split_axis=0, concat_axis=0, tiled=True)  6.72 us
    ppermute x1, starting transfers between devices, body(): from_right = lax.ppermute(beside(q_nodes[:SIDE]), columns, down)  3.8 us
  transfers between devices with their start and end apart: 4, of which 3 were waited for; matrix products, arithmetic and copies ran while one was open for 0% of the time, Pallas kernels for 1%

profile of v3, /device:TPU:1, one launch (start us, length us, event | category | flops | bytes accessed | tf_op | source)
XLA Modules:
  0.0 143.1 jit_solution(8776156838401526234)
XLA Ops:
  0.0 1.2 fusion.6
  1.2 0.1 pad.5.clone
  1.3 0.9 fusion.1
  2.2 2.1 %collective-permute-start = (f32[504,128]{1,0:T(8,128)S(1)}, f32[504,128]{1,0:T(8,128)S(1)}, u32[]{:S(2)}, u32[]{:S(2)}) collective-permute-start(f32[504,128]{1,0:T(8,128)S(1)} %get-tuple-element.24), channel_id=1, source_target_pairs={{0,8},{8,16},{16,24},{24,32},{32,40},{40,48},{48,56},{56,64},{64,7... | collective-permute-start | bytes 774152 | tf_op jit(solution)/shard_map/ppermute | solution.py:475
  4.3 3.8 %collective-permute-start.1 = (f32[504,128]{1,0:T(8,128)S(1)}, f32[504,128]{1,0:T(8,128)S(1)}, u32[]{:S(2)}, u32[]{:S(2)}) collective-permute-start(f32[504,128]{1,0:T(8,128)S(1)} %get-tuple-element.23), channel_id=1, source_target_pairs={{8,0},{16,8},{24,16},{32,24},{40,32},{48,40},{56,48},{64,56},{72,6... | collective-permute-start | bytes 774152 | tf_op jit(solution)/shard_map/ppermute | solution.py:476
  8.1 0.0 collective-permute-start.2
  8.1 0.0 copy-start.1
  8.1 1.4 copy-done.1
  9.5 1.6 %shard_map.73.inner_ref = f32[49,64,128]{2,1,0:T(8,128)S(1)} custom-call(f32[49,64,128]{2,1,0:T(8,128)S(1)} %bitcast.17, bf16[2,49,64,128]{3,2,1,0:T(8,128)(2,1)S(1)} %bitcast.10), custom_call_target="tpu_custom_call" | custom-call | tf_op jit(solution)/shard_map/pallas_call | solution.py:478
  11.2 1.8 %collective-permute-done.2.across_ref = f32[49,128]{1,0:T(8,128)S(1)} collective-permute-done((f32[49,128]{1,0:T(8,128)S(1)}, f32[49,128]{1,0:T(8,128)S(1)}, u32[]{:S(2)}, u32[]{:S(2)}) %collective-permute-start.2) | collective-permute-done | bytes 25120 | tf_op jit(solution)/shard_map/ppermute | solution.py:477
  13.0 0.9 collective-permute-done.left_ref
  13.9 1.4 shard_map.74
  15.3 6.7 %all-to-all-start = ((f32[8,392,128]{2,1,0:T(8,128)}), f32[8,392,128]{2,1,0:T(8,128)S(1)}, u32[]{:S(2)}, u32[]{:S(2)}) async-start(f32[8,392,128]{2,1,0:T(8,128)} %get-tuple-element.17), calls=%async_computation | async-start | bytes 3211264 | tf_op jit(solution)/shard_map/all_to_all | solution.py:489
  22.0 10.9 %all_gather.3.damp_ref = f32[896,128]{1,0:T(8,128)S(1)} all-gather(f32[224,128]{1,0:T(8,128)S(1)} %get-tuple-element.18), channel_id=1, replica_groups=mesh['y'=4,'x'=4,'z'=4,'core'=2] {'y'}, dimensions={0}, use_global_device_ids=true | all-gather | bytes 573440 | tf_op jit(solution)/shard_map/all_gather | solution.py:490
  32.8 10.2 %all-to-all-done.x_ref = f32[8,392,128]{2,1,0:T(8,128)S(1)} async-done(((f32[8,392,128]{2,1,0:T(8,128)}), f32[8,392,128]{2,1,0:T(8,128)S(1)}, u32[]{:S(2)}, u32[]{:S(2)}) %all-to-all-start) | async-done | bytes 1605664 | tf_op jit(solution)/shard_map/all_to_all | solution.py:489
  43.1 1.5 %shard_map.75 = f32[2432,128]{1,0:T(8,128)S(1)} custom-call(f32[8,392,128]{2,1,0:T(8,128)S(1)} %all-to-all-done.x_ref, bf16[384,512]{1,0:T(8,128)(2,1)S(1)} %copy-done.4, bf16[384,512]{1,0:T(8,128)(2,1)S(1)} %copy-done.5), custom_call_target="tpu_custom_call" | custom-call | tf_op jit(solution)/shard_map/pallas_call | solution.py:494
  44.5 28.1 %all_to_all.20 = f32[128,1,2432]{2,1,0:T(1,128)S(1)} all-to-all(f32[128,1,2432]{2,1,0:T(1,128)S(1)} %bitcast.14), channel_id=1, replica_groups=mesh['y'=4,'x'=4,'z'=4,'core'=2] {'core','z','y','x'}, dimensions={0} | all-to-all | bytes 2490368 | tf_op jit(solution)/shard_map/all_to_all | solution.py:495
  72.6 16.6 %shard_map.76 = f32[2432,128]{1,0:T(8,128)S(1)} custom-call(f32[3]{0:T(128)S(1)} %get-tuple-element.15.shift_ref, f32[3]{0:T(128)S(1)} %get-tuple-element.16.idle_ref, s32[1]{0:T(128)} %bitcast.place_ref, f32[2432,128]{1,0:T(8,128)S(1)} %bitcast.12, f32[896,128]{1,0:T(8,128)S(1)} %all_gather.3.damp_ref), custom_call_target="tpu_custom_call" | custom-call | tf_op jit(solution)/shard_map/pallas_call | solution.py:500
  89.3 0.0 copy-start.2
  89.3 0.0 copy-start.3
  89.3 25.3 %all_to_all.21 = f32[128,1,2432]{2,1,0:T(1,128)S(1)} all-to-all(f32[128,1,2432]{2,1,0:T(1,128)S(1)} %bitcast.13), channel_id=1, replica_groups=mesh['y'=4,'x'=4,'z'=4,'core'=2] {'core','z','y','x'}, dimensions={0} | all-to-all | bytes 2490368 | tf_op jit(solution)/shard_map/all_to_all | solution.py:504
  114.6 1.8 %shard_map.77 = f32[8,392,128]{2,1,0:T(8,128)S(1)} custom-call(f32[2432,128]{1,0:T(8,128)S(1)} %bitcast.15, bf16[512,384]{1,0:T(8,128)(2,1)S(1)} %copy-done.2, bf16[512,384]{1,0:T(8,128)(2,1)S(1)} %copy-done.3), custom_call_target="tpu_custom_call" | custom-call | tf_op jit(solution)/shard_map/pallas_call | solution.py:507
  116.4 25.5 %all_to_all.22.x_ref = f32[8,392,128]{2,1,0:T(8,128)S(1)} all-to-all(f32[8,392,128]{2,1,0:T(8,128)S(1)} %shard_map.77), channel_id=1, replica_groups=mesh['y'=4,'x'=4,'z'=4,'core'=2] {'z','core'}, dimensions={0} | all-to-all | bytes 3211264 | tf_op jit(solution)/shard_map/all_to_all | solution.py:510
  141.8 1.3 shard_map.78
  (13 shorter events, 0.0 us)
Async XLA Ops:
  0.0 8.1 %copy-start.6 = (f32[49,128]{1,0:T(8,128)S(1)}, f32[49,128]{1,0:T(8,128)}, u32[]{:S(2)}) copy-start(f32[49,128]{1,0:T(8,128)} %damp_ref.1) | copy-start | bytes 75268
  0.0 8.1 %copy-start = (bf16[2,64,49,128]{3,1,2,0:T(8,128)(2,1)S(1)}, bf16[2,64,49,128]{3,1,2,0:T(8,128)(2,1)}, u32[]{:S(2)}) copy-start(bf16[2,64,49,128]{3,1,2,0:T(8,128)(2,1)} %param.8) | copy-start | bytes 4816900
  2.2 11.7 %collective-permute-start = (f32[504,128]{1,0:T(8,128)S(1)}, f32[504,128]{1,0:T(8,128)S(1)}, u32[]{:S(2)}, u32[]{:S(2)}) collective-permute-start(f32[504,128]{1,0:T(8,128)S(1)} %get-tuple-element.24), channel_id=1, source_target_pairs={{0,8},{8,16},{16,24},{24,32},{32,40},{40,48},{48,56},{56,64},{64,7... | collective-permute-start | bytes 774152 | tf_op jit(solution)/shard_map/ppermute | solution.py:475
  4.3 9.6 %collective-permute-start.1 = (f32[504,128]{1,0:T(8,128)S(1)}, f32[504,128]{1,0:T(8,128)S(1)}, u32[]{:S(2)}, u32[]{:S(2)}) collective-permute-start(f32[504,128]{1,0:T(8,128)S(1)} %get-tuple-element.23), channel_id=1, source_target_pairs={{8,0},{16,8},{24,16},{32,24},{40,32},{48,40},{56,48},{64,56},{72,6... | collective-permute-start | bytes 774152 | tf_op jit(solution)/shard_map/ppermute | solution.py:476
  8.1 4.9 %collective-permute-start.2 = (f32[49,128]{1,0:T(8,128)S(1)}, f32[49,128]{1,0:T(8,128)S(1)}, u32[]{:S(2)}, u32[]{:S(2)}) collective-permute-start(f32[49,128]{1,0:T(8,128)S(1)} %copy-done.6), channel_id=1, source_target_pairs={{0,16},{8,24},{16,0},{24,8},{1,17},{9,25},{17,1},{25,9},{2,18},{10... | collective-permute-start | bytes 75272 | tf_op jit(solution)/shard_map/ppermute | solution.py:477
  8.1 1.4 copy-start.1
  15.3 27.8 %copy-start.4 = (bf16[384,512]{1,0:T(8,128)(2,1)S(1)}, bf16[384,512]{1,0:T(8,128)(2,1)}, u32[]{:S(2)}) copy-start(bf16[384,512]{1,0:T(8,128)(2,1)} %constant.48.clone.high_ref) | copy-start | bytes 1179652
  15.3 27.8 %copy-start.5 = (bf16[384,512]{1,0:T(8,128)(2,1)S(1)}, bf16[384,512]{1,0:T(8,128)(2,1)}, u32[]{:S(2)}) copy-start(bf16[384,512]{1,0:T(8,128)(2,1)} %constant.49.clone.low_ref) | copy-start | bytes 1179652
  15.3 27.8 %all-to-all-start = ((f32[8,392,128]{2,1,0:T(8,128)}), f32[8,392,128]{2,1,0:T(8,128)S(1)}, u32[]{:S(2)}, u32[]{:S(2)}) async-start(f32[8,392,128]{2,1,0:T(8,128)} %get-tuple-element.17), calls=%async_computation | async-start | bytes 3211264 | tf_op jit(solution)/shard_map/all_to_all | solution.py:489
  89.3 25.3 %copy-start.2 = (bf16[512,384]{1,0:T(8,128)(2,1)S(1)}, bf16[512,384]{1,0:T(8,128)(2,1)}, u32[]{:S(2)}) copy-start(bf16[512,384]{1,0:T(8,128)(2,1)} %constant.50.clone.high_ref) | copy-start | bytes 1179652
  89.3 25.3 %copy-start.3 = (bf16[512,384]{1,0:T(8,128)(2,1)S(1)}, bf16[512,384]{1,0:T(8,128)(2,1)}, u32[]{:S(2)}) copy-start(bf16[512,384]{1,0:T(8,128)(2,1)} %constant.51.clone.low_ref) | copy-start | bytes 1179652

commit v4 on v3

--- a/solution.py
+++ b/solution.py
@@ -423,21 +423,22 @@
         spread([fresh[m] / (norm[m] + idle_ref[m]) for m in range(M_DEV)])
         return tuple(fresh)
 
-    lax.fori_loop(0, ITERS, iteration, tuple(totals()))
-
-    def finish(mode, carry):
-        base = mode * NODES
+    norm = lax.fori_loop(0, ITERS - 1, iteration, tuple(totals()))
+    lax.fori_loop(0, M_DEV, apply, 0)
+    curve = totals()
+    spread([norm[m] / (curve[m] + idle_ref[m]) for m in range(M_DEV)])
+
+    def solved(mode, n):
+        return x_ref[mode * NODES + n] + ratio_ref[mode] * p_ref[mode * NODES + n]
+
+    for mode in range(M_DEV):
         for n in range(NODES - 1):
-            start = first_row(n // GROUPS) + n % GROUPS
-            store(start + mode * GROUPS, stride, x_ref[base + n])
-        return carry
-
-    lax.fori_loop(0, M_DEV, finish, 0)
+            store(first_row(n // GROUPS) + n % GROUPS + mode * GROUPS, stride, solved(mode, n))
+    rests = [solved(mode, NODES - 1) for mode in range(M_DEV)]
     for s in range(N_SPAN):
         own = zero
         for mode in range(M_DEV):
-            rest = turn(x_ref[mode * NODES + NODES - 1], (mode - s) * PIECE)
-            own = jnp.where(piece == mode, rest, own)
+            own = jnp.where(piece == mode, turn(rests[mode], (mode - s) * PIECE), own)
         store(first_row(s) + PAIR - 1, stride, own)
 
 
@@ -467,10 +468,12 @@
     down = [(j, i) for i, j in up]
     q_nodes = jnp.transpose(velocity_q, (1, 0, 2))
     a_nodes = jnp.transpose(advecting, (0, 2, 1, 3))
-    blank = jnp.zeros((PADDED - NODES, EY), jnp.float32)
 
     def beside(face):
-        return jnp.concatenate([face.reshape(SIDE * PL_DEV, EY), damping, blank])
+        faces = SIDE * PL_DEV
+        return jnp.pad(face.reshape(faces, EY), ((0, PADDED), (0, 0))) + jnp.pad(
+            damping, ((faces, PADDED - NODES), (0, 0))
+        )
 
     from_left = lax.ppermute(beside(q_nodes[NODES - SIDE :]), columns, up)
     from_right = lax.ppermute(beside(q_nodes[:SIDE]), columns, down)

time: 143 us -> 143 us (level)
  no operation moved by 1% of the time
where the time goes in v4:
time: 143 us
  blocking collectives  89.7 us (63%)
  Pallas kernels  24 us (17%)
  waiting for transfers between devices  12.9 us (9%)
  starting transfers between devices  12.6 us (9%)
  local copies, waits for them, and re-layouts  2.64 us (2%)
    all_to_all x1, blocking collectives, body(): lax.all_to_all(spectra.reshape(N_DEV, 1, PAIR * EY), everyone, split_axis...  28.1 us
    all_to_all x1, blocking collectives, body(): lax.all_to_all(physical, span, split_axis=0, concat_axis=0, tiled=True)  25.5 us
    all_to_all x1, blocking collectives, body(): lax.all_to_all(solved.reshape(N_DEV, 1, PAIR * EY), everyone, split_axis=...  25.3 us
    pallas_call x1, Pallas kernels, body(): call(solve_kernel, (N_DEV * PAIR, EY), scratch=(field,) * 5 + (part,) * 2...  16.5 us
    all_gather x1, blocking collectives, body(): damp_nodes = lax.all_gather(damp_row, 'y', axis=0, tiled=True)  10.9 us
    all_to_all x1, waiting for transfers between devices, body(): lax.all_to_all(forcing, span, split_axis=0, concat_axis=0, tiled=True)  10.2 us
    all_to_all x1, starting transfers between devices, body(): lax.all_to_all(forcing, span, split_axis=0, concat_axis=0, tiled=True)  6.72 us
    ppermute x1, starting transfers between devices, body(): from_right = lax.ppermute(beside(q_nodes[:SIDE]), columns, down)  3.8 us
  transfers between devices with their start and end apart: 4, of which 3 were waited for; matrix products, arithmetic and copies ran while one was open for 0% of the time, Pallas kernels for 1%

profile of v4, /device:TPU:1, one launch (start us, length us, event | category | flops | bytes accessed | tf_op | source)
XLA Modules:
  0.0 142.8 jit_solution(9817022961012887654)
XLA Ops:
  0.0 1.2 fusion.4
  1.2 0.8 pad_add_fusion
  2.0 2.1 %collective-permute-start = (f32[504,128]{1,0:T(8,128)S(1)}, f32[504,128]{1,0:T(8,128)S(1)}, u32[]{:S(2)}, u32[]{:S(2)}) collective-permute-start(f32[504,128]{1,0:T(8,128)S(1)} %get-tuple-element.24), channel_id=1, source_target_pairs={{0,8},{8,16},{16,24},{24,32},{32,40},{40,48},{48,56},{56,64},{64,7... | collective-permute-start | bytes 774152 | tf_op jit(solution)/shard_map/ppermute | solution.py:478
  4.1 3.8 %collective-permute-start.1 = (f32[504,128]{1,0:T(8,128)S(1)}, f32[504,128]{1,0:T(8,128)S(1)}, u32[]{:S(2)}, u32[]{:S(2)}) collective-permute-start(f32[504,128]{1,0:T(8,128)S(1)} %get-tuple-element.23), channel_id=1, source_target_pairs={{8,0},{16,8},{24,16},{32,24},{40,32},{48,40},{56,48},{64,56},{72,6... | collective-permute-start | bytes 774152 | tf_op jit(solution)/shard_map/ppermute | solution.py:479
  7.9 0.0 collective-permute-start.2
  7.9 0.0 copy-start.1
  7.9 1.4 copy-done.1
  9.4 1.6 %shard_map.73.inner_ref = f32[49,64,128]{2,1,0:T(8,128)S(1)} custom-call(f32[49,64,128]{2,1,0:T(8,128)S(1)} %bitcast.17, bf16[2,49,64,128]{3,2,1,0:T(8,128)(2,1)S(1)} %bitcast.10), custom_call_target="tpu_custom_call" | custom-call | tf_op jit(solution)/shard_map/pallas_call | solution.py:481
  11.0 1.8 %collective-permute-done.2.across_ref = f32[49,128]{1,0:T(8,128)S(1)} collective-permute-done((f32[49,128]{1,0:T(8,128)S(1)}, f32[49,128]{1,0:T(8,128)S(1)}, u32[]{:S(2)}, u32[]{:S(2)}) %collective-permute-start.2) | collective-permute-done | bytes 25120 | tf_op jit(solution)/shard_map/ppermute | solution.py:480
  12.8 0.9 collective-permute-done.left_ref
  13.7 0.0 collective-permute-done.1.right_ref
  13.7 1.4 shard_map.74
  15.1 6.7 %all-to-all-start = ((f32[8,392,128]{2,1,0:T(8,128)}), f32[8,392,128]{2,1,0:T(8,128)S(1)}, u32[]{:S(2)}, u32[]{:S(2)}) async-start(f32[8,392,128]{2,1,0:T(8,128)} %get-tuple-element.17), calls=%async_computation | async-start | bytes 3211264 | tf_op jit(solution)/shard_map/all_to_all | solution.py:492
  21.8 10.9 %all_gather.3.damp_ref = f32[896,128]{1,0:T(8,128)S(1)} all-gather(f32[224,128]{1,0:T(8,128)S(1)} %get-tuple-element.18), channel_id=1, replica_groups=mesh['y'=4,'x'=4,'z'=4,'core'=2] {'y'}, dimensions={0}, use_global_device_ids=true | all-gather | bytes 573440 | tf_op jit(solution)/shard_map/all_gather | solution.py:493
  32.7 10.2 %all-to-all-done.x_ref = f32[8,392,128]{2,1,0:T(8,128)S(1)} async-done(((f32[8,392,128]{2,1,0:T(8,128)}), f32[8,392,128]{2,1,0:T(8,128)S(1)}, u32[]{:S(2)}, u32[]{:S(2)}) %all-to-all-start) | async-done | bytes 1605664 | tf_op jit(solution)/shard_map/all_to_all | solution.py:492
  42.9 1.5 %shard_map.75 = f32[2432,128]{1,0:T(8,128)S(1)} custom-call(f32[8,392,128]{2,1,0:T(8,128)S(1)} %all-to-all-done.x_ref, bf16[384,512]{1,0:T(8,128)(2,1)S(1)} %copy-done.4, bf16[384,512]{1,0:T(8,128)(2,1)S(1)} %copy-done.5), custom_call_target="tpu_custom_call" | custom-call | tf_op jit(solution)/shard_map/pallas_call | solution.py:497
  44.3 28.1 %all_to_all.20 = f32[128,1,2432]{2,1,0:T(1,128)S(1)} all-to-all(f32[128,1,2432]{2,1,0:T(1,128)S(1)} %bitcast.14), channel_id=1, replica_groups=mesh['y'=4,'x'=4,'z'=4,'core'=2] {'core','z','y','x'}, dimensions={0} | all-to-all | bytes 2490368 | tf_op jit(solution)/shard_map/all_to_all | solution.py:498
  72.5 16.5 %shard_map.76 = f32[2432,128]{1,0:T(8,128)S(1)} custom-call(f32[3]{0:T(128)S(1)} %get-tuple-element.15.shift_ref, f32[3]{0:T(128)S(1)} %get-tuple-element.16.idle_ref, s32[1]{0:T(128)} %bitcast.place_ref, f32[2432,128]{1,0:T(8,128)S(1)} %bitcast.12, f32[896,128]{1,0:T(8,128)S(1)} %all_gather.3.damp_ref), custom_call_target="tpu_custom_call" | custom-call | tf_op jit(solution)/shard_map/pallas_call | solution.py:503
  89.0 0.0 copy-start.2
  89.0 0.0 copy-start.3
  89.0 25.3 %all_to_all.21 = f32[128,1,2432]{2,1,0:T(1,128)S(1)} all-to-all(f32[128,1,2432]{2,1,0:T(1,128)S(1)} %bitcast.13), channel_id=1, replica_groups=mesh['y'=4,'x'=4,'z'=4,'core'=2] {'core','z','y','x'}, dimensions={0} | all-to-all | bytes 2490368 | tf_op jit(solution)/shard_map/all_to_all | solution.py:507
  114.3 1.8 %shard_map.77 = f32[8,392,128]{2,1,0:T(8,128)S(1)} custom-call(f32[2432,128]{1,0:T(8,128)S(1)} %bitcast.15, bf16[512,384]{1,0:T(8,128)(2,1)S(1)} %copy-done.2, bf16[512,384]{1,0:T(8,128)(2,1)S(1)} %copy-done.3), custom_call_target="tpu_custom_call" | custom-call | tf_op jit(solution)/shard_map/pallas_call | solution.py:510
  116.1 25.5 %all_to_all.22.x_ref = f32[8,392,128]{2,1,0:T(8,128)S(1)} all-to-all(f32[8,392,128]{2,1,0:T(8,128)S(1)} %shard_map.77), channel_id=1, replica_groups=mesh['y'=4,'x'=4,'z'=4,'core'=2] {'z','core'}, dimensions={0} | all-to-all | bytes 3211264 | tf_op jit(solution)/shard_map/all_to_all | solution.py:513
  141.5 1.3 shard_map.78
  (11 shorter events, 0.0 us)
Async XLA Ops:
  0.0 7.9 %copy-start.6 = (f32[49,128]{1,0:T(8,128)S(1)}, f32[49,128]{1,0:T(8,128)}, u32[]{:S(2)}) copy-start(f32[49,128]{1,0:T(8,128)} %damp_ref.1) | copy-start | bytes 75268
  0.0 7.9 %copy-start = (bf16[2,64,49,128]{3,1,2,0:T(8,128)(2,1)S(1)}, bf16[2,64,49,128]{3,1,2,0:T(8,128)(2,1)}, u32[]{:S(2)}) copy-start(bf16[2,64,49,128]{3,1,2,0:T(8,128)(2,1)} %param.8) | copy-start | bytes 4816900
  2.0 11.7 %collective-permute-start = (f32[504,128]{1,0:T(8,128)S(1)}, f32[504,128]{1,0:T(8,128)S(1)}, u32[]{:S(2)}, u32[]{:S(2)}) collective-permute-start(f32[504,128]{1,0:T(8,128)S(1)} %get-tuple-element.24), channel_id=1, source_target_pairs={{0,8},{8,16},{16,24},{24,32},{32,40},{40,48},{48,56},{56,64},{64,7... | collective-permute-start | bytes 774152 | tf_op jit(solution)/shard_map/ppermute | solution.py:478
  4.1 9.6 %collective-permute-start.1 = (f32[504,128]{1,0:T(8,128)S(1)}, f32[504,128]{1,0:T(8,128)S(1)}, u32[]{:S(2)}, u32[]{:S(2)}) collective-permute-start(f32[504,128]{1,0:T(8,128)S(1)} %get-tuple-element.23), channel_id=1, source_target_pairs={{8,0},{16,8},{24,16},{32,24},{40,32},{48,40},{56,48},{64,56},{72,6... | collective-permute-start | bytes 774152 | tf_op jit(solution)/shard_map/ppermute | solution.py:479
  7.9 4.9 %collective-permute-start.2 = (f32[49,128]{1,0:T(8,128)S(1)}, f32[49,128]{1,0:T(8,128)S(1)}, u32[]{:S(2)}, u32[]{:S(2)}) collective-permute-start(f32[49,128]{1,0:T(8,128)S(1)} %copy-done.6), channel_id=1, source_target_pairs={{0,16},{8,24},{16,0},{24,8},{1,17},{9,25},{17,1},{25,9},{2,18},{10... | collective-permute-start | bytes 75272 | tf_op jit(solution)/shard_map/ppermute | solution.py:480
  7.9 1.4 copy-start.1
  15.1 27.8 %copy-start.4 = (bf16[384,512]{1,0:T(8,128)(2,1)S(1)}, bf16[384,512]{1,0:T(8,128)(2,1)}, u32[]{:S(2)}) copy-start(bf16[384,512]{1,0:T(8,128)(2,1)} %constant.49.clone.high_ref) | copy-start | bytes 1179652
  15.1 27.8 %copy-start.5 = (bf16[384,512]{1,0:T(8,128)(2,1)S(1)}, bf16[384,512]{1,0:T(8,128)(2,1)}, u32[]{:S(2)}) copy-start(bf16[384,512]{1,0:T(8,128)(2,1)} %constant.50.clone.low_ref) | copy-start | bytes 1179652
  15.1 27.8 %all-to-all-start = ((f32[8,392,128]{2,1,0:T(8,128)}), f32[8,392,128]{2,1,0:T(8,128)S(1)}, u32[]{:S(2)}, u32[]{:S(2)}) async-start(f32[8,392,128]{2,1,0:T(8,128)} %get-tuple-element.17), calls=%async_computation | async-start | bytes 3211264 | tf_op jit(solution)/shard_map/all_to_all | solution.py:492
  89.0 25.3 %copy-start.2 = (bf16[512,384]{1,0:T(8,128)(2,1)S(1)}, bf16[512,384]{1,0:T(8,128)(2,1)}, u32[]{:S(2)}) copy-start(bf16[512,384]{1,0:T(8,128)(2,1)} %constant.51.clone.high_ref) | copy-start | bytes 1179652
  89.0 25.3 %copy-start.3 = (bf16[512,384]{1,0:T(8,128)(2,1)S(1)}, bf16[512,384]{1,0:T(8,128)(2,1)}, u32[]{:S(2)}) copy-start(bf16[512,384]{1,0:T(8,128)(2,1)} %constant.52.clone.low_ref) | copy-start | bytes 1179652

commit v5 on v4

--- a/solution.py
+++ b/solution.py
@@ -343,33 +343,25 @@
         odd = jnp.where(wrap_odd, pltpu.roll(odd, half - 2, 0), odd)
         return jnp.concatenate([even, odd], axis=0)
 
-    def begin(mode, carry):
-        shift = shift_ref[mode]
-        base = mode * NODES
-        norm = zero
-        for n in range(NODES):
-            w = np.float32(W[n // SIDE] * W[n % SIDE])
+    norms = [zero] * M_DEV
+    rests = [load(b_ref, first_row(s) + PAIR - 1, stride) for s in range(N_SPAN)]
+    for n in range(NODES):
+        w = np.float32(W[n // SIDE] * W[n % SIDE])
+        damp = w * damp_of(n)
+        for mode in range(M_DEV):
             if n < NODES - 1:
-                start = first_row(n // GROUPS) + n % GROUPS
-                rows = load(b_ref, start + mode * GROUPS, stride)
+                rows = load(b_ref, first_row(n // GROUPS) + n % GROUPS + mode * GROUPS, stride)
             else:
-                rows = zero
-                for s in range(N_SPAN):
-                    rest = load(b_ref, first_row(s) + PAIR - 1, stride)
-                    own = pltpu.roll(rest, lax.rem(s * PIECE + EY - mode * PIECE, EY), 1)
-                    rows = jnp.where(piece == s, own, rows)
-            damp = damp_of(n)
+                rows = pack(rests, [(s - mode) * PIECE for s in range(N_SPAN)])
             rhs = w * rows
-            r_ref[base + n] = rhs
-            p_ref[base + n] = zero
-            x_ref[base + n] = zero
-            mass_ref[base + n] = w * (damp + shift)
-            norm = norm + rhs * rhs
-        part_ref[mode] = norm
+            r_ref[mode * NODES + n] = rhs
+            p_ref[mode * NODES + n] = zero
+            x_ref[mode * NODES + n] = zero
+            mass_ref[mode * NODES + n] = damp + w * shift_ref[mode]
+            norms[mode] = norms[mode] + rhs * rhs
+    for mode in range(M_DEV):
+        part_ref[mode] = norms[mode]
         ratio_ref[mode] = zero
-        return carry
-
-    lax.fori_loop(0, M_DEV, begin, 0)
 
     def apply(mode, carry):
         base = mode * NODES

time: 143 us -> 143 us (level)
  no operation moved by 1% of the time
where the time goes in v5:
time: 143 us; the launch traced here: 142 us
  blocking collectives  89.7 us (63%)
  Pallas kernels  23.5 us (16%)
  waiting for transfers between devices  12.9 us (9%)
  starting transfers between devices  12.6 us (9%)
  local copies, waits for them, and re-layouts  2.64 us (2%)
    all_to_all x1, blocking collectives, body(): lax.all_to_all(spectra.reshape(N_DEV, 1, PAIR * EY), everyone, split_axis...  28.1 us
    all_to_all x1, blocking collectives, body(): lax.all_to_all(physical, span, split_axis=0, concat_axis=0, tiled=True)  25.5 us
    all_to_all x1, blocking collectives, body(): lax.all_to_all(solved.reshape(N_DEV, 1, PAIR * EY), everyone, split_axis=...  25.3 us
    pallas_call x1, Pallas kernels, body(): call(solve_kernel, (N_DEV * PAIR, EY), scratch=(field,) * 5 + (part,) * 2...  16.1 us
    all_gather x1, blocking collectives, body(): damp_nodes = lax.all_gather(damp_row, 'y', axis=0, tiled=True)  10.9 us
    all_to_all x1, waiting for transfers between devices, body(): lax.all_to_all(forcing, span, split_axis=0, concat_axis=0, tiled=True)  10.2 us
    all_to_all x1, starting transfers between devices, body(): lax.all_to_all(forcing, span, split_axis=0, concat_axis=0, tiled=True)  6.72 us
    ppermute x1, starting transfers between devices, body(): from_right = lax.ppermute(beside(q_nodes[:SIDE]), columns, down)  3.8 us
  transfers between devices with their start and end apart: 4, of which 3 were waited for; matrix products, arithmetic and copies ran while one was open for 0% of the time, Pallas kernels for 1%

profile of v5, /device:TPU:1, one launch (start us, length us, event | category | flops | bytes accessed | tf_op | source)
XLA Modules:
  0.0 142.4 jit_solution(13091029143460920238)
XLA Ops:
  0.0 1.2 fusion.4
  1.2 0.8 pad_add_fusion
  2.0 2.1 %collective-permute-start = (f32[504,128]{1,0:T(8,128)S(1)}, f32[504,128]{1,0:T(8,128)S(1)}, u32[]{:S(2)}, u32[]{:S(2)}) collective-permute-start(f32[504,128]{1,0:T(8,128)S(1)} %get-tuple-element.24), channel_id=1, source_target_pairs={{0,8},{8,16},{16,24},{24,32},{32,40},{40,48},{48,56},{56,64},{64,7... | collective-permute-start | bytes 774152 | tf_op jit(solution)/shard_map/ppermute | solution.py:470
  4.1 3.8 %collective-permute-start.1 = (f32[504,128]{1,0:T(8,128)S(1)}, f32[504,128]{1,0:T(8,128)S(1)}, u32[]{:S(2)}, u32[]{:S(2)}) collective-permute-start(f32[504,128]{1,0:T(8,128)S(1)} %get-tuple-element.23), channel_id=1, source_target_pairs={{8,0},{16,8},{24,16},{32,24},{40,32},{48,40},{56,48},{64,56},{72,6... | collective-permute-start | bytes 774152 | tf_op jit(solution)/shard_map/ppermute | solution.py:471
  7.9 0.0 collective-permute-start.2
  7.9 0.0 copy-start.1
  7.9 1.4 copy-done.1
  9.4 1.6 %shard_map.73.inner_ref = f32[49,64,128]{2,1,0:T(8,128)S(1)} custom-call(f32[49,64,128]{2,1,0:T(8,128)S(1)} %bitcast.17, bf16[2,49,64,128]{3,2,1,0:T(8,128)(2,1)S(1)} %bitcast.10), custom_call_target="tpu_custom_call" | custom-call | tf_op jit(solution)/shard_map/pallas_call | solution.py:473
  11.0 1.8 %collective-permute-done.2.across_ref = f32[49,128]{1,0:T(8,128)S(1)} collective-permute-done((f32[49,128]{1,0:T(8,128)S(1)}, f32[49,128]{1,0:T(8,128)S(1)}, u32[]{:S(2)}, u32[]{:S(2)}) %collective-permute-start.2) | collective-permute-done | bytes 25120 | tf_op jit(solution)/shard_map/ppermute | solution.py:472
  12.8 0.9 collective-permute-done.left_ref
  13.7 0.0 collective-permute-done.1.right_ref
  13.7 1.4 shard_map.74
  15.1 6.7 %all-to-all-start = ((f32[8,392,128]{2,1,0:T(8,128)}), f32[8,392,128]{2,1,0:T(8,128)S(1)}, u32[]{:S(2)}, u32[]{:S(2)}) async-start(f32[8,392,128]{2,1,0:T(8,128)} %get-tuple-element.17), calls=%async_computation | async-start | bytes 3211264 | tf_op jit(solution)/shard_map/all_to_all | solution.py:484
  21.8 10.9 %all_gather.3.damp_ref = f32[896,128]{1,0:T(8,128)S(1)} all-gather(f32[224,128]{1,0:T(8,128)S(1)} %get-tuple-element.18), channel_id=1, replica_groups=mesh['y'=4,'x'=4,'z'=4,'core'=2] {'y'}, dimensions={0}, use_global_device_ids=true | all-gather | bytes 573440 | tf_op jit(solution)/shard_map/all_gather | solution.py:485
  32.7 10.2 %all-to-all-done.x_ref = f32[8,392,128]{2,1,0:T(8,128)S(1)} async-done(((f32[8,392,128]{2,1,0:T(8,128)}), f32[8,392,128]{2,1,0:T(8,128)S(1)}, u32[]{:S(2)}, u32[]{:S(2)}) %all-to-all-start) | async-done | bytes 1605664 | tf_op jit(solution)/shard_map/all_to_all | solution.py:484
  42.9 1.5 %shard_map.75 = f32[2432,128]{1,0:T(8,128)S(1)} custom-call(f32[8,392,128]{2,1,0:T(8,128)S(1)} %all-to-all-done.x_ref, bf16[384,512]{1,0:T(8,128)(2,1)S(1)} %copy-done.4, bf16[384,512]{1,0:T(8,128)(2,1)S(1)} %copy-done.5), custom_call_target="tpu_custom_call" | custom-call | tf_op jit(solution)/shard_map/pallas_call | solution.py:489
  44.3 28.1 %all_to_all.20 = f32[128,1,2432]{2,1,0:T(1,128)S(1)} all-to-all(f32[128,1,2432]{2,1,0:T(1,128)S(1)} %bitcast.14), channel_id=1, replica_groups=mesh['y'=4,'x'=4,'z'=4,'core'=2] {'core','z','y','x'}, dimensions={0} | all-to-all | bytes 2490368 | tf_op jit(solution)/shard_map/all_to_all | solution.py:490
  72.5 16.1 %shard_map.76 = f32[2432,128]{1,0:T(8,128)S(1)} custom-call(f32[3]{0:T(128)S(1)} %get-tuple-element.15.shift_ref, f32[3]{0:T(128)S(1)} %get-tuple-element.16.idle_ref, s32[1]{0:T(128)} %bitcast.place_ref, f32[2432,128]{1,0:T(8,128)S(1)} %bitcast.12, f32[896,128]{1,0:T(8,128)S(1)} %all_gather.3.damp_ref), custom_call_target="tpu_custom_call" | custom-call | tf_op jit(solution)/shard_map/pallas_call | solution.py:495
  88.5 0.0 copy-start.2
  88.6 0.0 copy-start.3
  88.6 25.3 %all_to_all.21 = f32[128,1,2432]{2,1,0:T(1,128)S(1)} all-to-all(f32[128,1,2432]{2,1,0:T(1,128)S(1)} %bitcast.13), channel_id=1, replica_groups=mesh['y'=4,'x'=4,'z'=4,'core'=2] {'core','z','y','x'}, dimensions={0} | all-to-all | bytes 2490368 | tf_op jit(solution)/shard_map/all_to_all | solution.py:499
  113.9 1.8 %shard_map.77 = f32[8,392,128]{2,1,0:T(8,128)S(1)} custom-call(f32[2432,128]{1,0:T(8,128)S(1)} %bitcast.15, bf16[512,384]{1,0:T(8,128)(2,1)S(1)} %copy-done.2, bf16[512,384]{1,0:T(8,128)(2,1)S(1)} %copy-done.3), custom_call_target="tpu_custom_call" | custom-call | tf_op jit(solution)/shard_map/pallas_call | solution.py:502
  115.6 25.5 %all_to_all.22.x_ref = f32[8,392,128]{2,1,0:T(8,128)S(1)} all-to-all(f32[8,392,128]{2,1,0:T(8,128)S(1)} %shard_map.77), channel_id=1, replica_groups=mesh['y'=4,'x'=4,'z'=4,'core'=2] {'z','core'}, dimensions={0} | all-to-all | bytes 3211264 | tf_op jit(solution)/shard_map/all_to_all | solution.py:505
  141.1 1.3 shard_map.78
  (11 shorter events, 0.0 us)
Async XLA Ops:
  0.0 7.9 %copy-start.6 = (f32[49,128]{1,0:T(8,128)S(1)}, f32[49,128]{1,0:T(8,128)}, u32[]{:S(2)}) copy-start(f32[49,128]{1,0:T(8,128)} %damp_ref.1) | copy-start | bytes 75268
  0.0 7.9 %copy-start = (bf16[2,64,49,128]{3,1,2,0:T(8,128)(2,1)S(1)}, bf16[2,64,49,128]{3,1,2,0:T(8,128)(2,1)}, u32[]{:S(2)}) copy-start(bf16[2,64,49,128]{3,1,2,0:T(8,128)(2,1)} %param.8) | copy-start | bytes 4816900
  2.0 11.7 %collective-permute-start = (f32[504,128]{1,0:T(8,128)S(1)}, f32[504,128]{1,0:T(8,128)S(1)}, u32[]{:S(2)}, u32[]{:S(2)}) collective-permute-start(f32[504,128]{1,0:T(8,128)S(1)} %get-tuple-element.24), channel_id=1, source_target_pairs={{0,8},{8,16},{16,24},{24,32},{32,40},{40,48},{48,56},{56,64},{64,7... | collective-permute-start | bytes 774152 | tf_op jit(solution)/shard_map/ppermute | solution.py:470
  4.1 9.6 %collective-permute-start.1 = (f32[504,128]{1,0:T(8,128)S(1)}, f32[504,128]{1,0:T(8,128)S(1)}, u32[]{:S(2)}, u32[]{:S(2)}) collective-permute-start(f32[504,128]{1,0:T(8,128)S(1)} %get-tuple-element.23), channel_id=1, source_target_pairs={{8,0},{16,8},{24,16},{32,24},{40,32},{48,40},{56,48},{64,56},{72,6... | collective-permute-start | bytes 774152 | tf_op jit(solution)/shard_map/ppermute | solution.py:471
  7.9 4.9 %collective-permute-start.2 = (f32[49,128]{1,0:T(8,128)S(1)}, f32[49,128]{1,0:T(8,128)S(1)}, u32[]{:S(2)}, u32[]{:S(2)}) collective-permute-start(f32[49,128]{1,0:T(8,128)S(1)} %copy-done.6), channel_id=1, source_target_pairs={{0,16},{8,24},{16,0},{24,8},{1,17},{9,25},{17,1},{25,9},{2,18},{10... | collective-permute-start | bytes 75272 | tf_op jit(solution)/shard_map/ppermute | solution.py:472
  7.9 1.4 copy-start.1
  15.1 27.8 %copy-start.4 = (bf16[384,512]{1,0:T(8,128)(2,1)S(1)}, bf16[384,512]{1,0:T(8,128)(2,1)}, u32[]{:S(2)}) copy-start(bf16[384,512]{1,0:T(8,128)(2,1)} %constant.49.clone.high_ref) | copy-start | bytes 1179652
  15.1 27.8 %copy-start.5 = (bf16[384,512]{1,0:T(8,128)(2,1)S(1)}, bf16[384,512]{1,0:T(8,128)(2,1)}, u32[]{:S(2)}) copy-start(bf16[384,512]{1,0:T(8,128)(2,1)} %constant.50.clone.low_ref) | copy-start | bytes 1179652
  15.1 27.8 %all-to-all-start = ((f32[8,392,128]{2,1,0:T(8,128)}), f32[8,392,128]{2,1,0:T(8,128)S(1)}, u32[]{:S(2)}, u32[]{:S(2)}) async-start(f32[8,392,128]{2,1,0:T(8,128)} %get-tuple-element.17), calls=%async_computation | async-start | bytes 3211264 | tf_op jit(solution)/shard_map/all_to_all | solution.py:484
  88.5 25.3 %copy-start.2 = (bf16[512,384]{1,0:T(8,128)(2,1)S(1)}, bf16[512,384]{1,0:T(8,128)(2,1)}, u32[]{:S(2)}) copy-start(bf16[512,384]{1,0:T(8,128)(2,1)} %constant.51.clone.high_ref) | copy-start | bytes 1179652
  88.6 25.3 %copy-start.3 = (bf16[512,384]{1,0:T(8,128)(2,1)S(1)}, bf16[512,384]{1,0:T(8,128)(2,1)}, u32[]{:S(2)}) copy-start(bf16[512,384]{1,0:T(8,128)(2,1)} %constant.52.clone.low_ref) | copy-start | bytes 1179652
